TPU v7x, 1024 devices: a whole 4x8x16 slice. The times are simulated.
1024 devices in a mesh: dp: 16 (over x, z_lo), shard: 64 (over z_hi, y, core).
Axes of the slice: x: 4, y: 8, z: 16 (z_hi: 4, z_lo: 4; z = z_hi * 4 + z_lo), core: 2. Of those that a mesh axis runs over, the one named last changes fastest.
Arguments:
- features: bfloat16 [2048, 4096], P('dp'), may hold values from -40 to 40
- out_grads: bfloat16 [2048, 16384], P('dp', 'shard'), may hold values from -120 to 120
- token_counts: int32 [16], replicated, may hold values from 42 to 128, as said below
- owner_order: int32 [32, 8], replicated, may hold values from 0 to 7, each once within a row
- moment: float32 [16384, 4096], P('shard', 'dp'), may hold values from -40 to 40
- second: float32 [16384, 4096], P('shard', 'dp'), may hold values from 0.03 to 1
- left_stat: float32 [64, 16, 128, 512], P('shard', 'dp'), may hold values from -0.5 to 2.5, as said below
- right_stat: float32 [64, 16, 128, 512], P('shard', 'dp'), may hold values from -0.5 to 2.5, as said below
- left_root: float32 [64, 16, 128, 512], P('shard', 'dp'), may hold values from -0.5 to 2, as said below
- right_root: float32 [64, 16, 128, 512], P('shard', 'dp'), may hold values from -0.5 to 2, as said below
Outputs:
- update: float32 [16384, 4096], P('shard', 'dp')
- new_moment: float32 [16384, 4096], P('shard', 'dp')
- new_second: float32 [16384, 4096], P('shard', 'dp')
- next_left: float32 [64, 16, 128, 512], P('shard', 'dp')
- next_right: float32 [64, 16, 128, 512], P('shard', 'dp')
Inputs may be any that keep to these rules, and one draw needn't show every extreme that they name: The first token_counts[g] tokens of group g are live, the others padding. `owner_order`: each row is a permutation of 0 to 7. `left_stat`: each block's matrix is symmetric. `right_stat`: each block's matrix is symmetric. `left_root`: each block's matrix is symmetric. `right_root`: each block's matrix is symmetric.
All inputs are finite; a program needn't handle non-finite values.
Results may differ from a plain program's by a relative error of at most 0.00035.
Values may be sent and summed in bfloat16 or wider, within the bound.
No kernel may reach another device: no remote copies, remote signals or barrier semaphores. Data moves between devices by JAX's collectives and lax.ppermute only.
A program may use at most 32 MiB of HBM per device.

v0:
```python
import jax
import jax.numpy as jnp
from jax import lax
from jax.experimental import pallas as pl
from jax.experimental.pallas import tpu as pltpu
from jax.sharding import Mesh, PartitionSpec as P

DP = ("x", "zl")
SHARD = ("zh", "y", "c")
SIZES = (4, 4, 4, 8, 2)
VMEM_LIMIT = 40 * 1024 * 1024


def partner(value, axis):
    return lax.ppermute(value, axis, [(i, i ^ 1) for i in range(lax.axis_size(axis))])


def split(value):
    high = value.astype(jnp.bfloat16)
    return high, (value - high.astype(jnp.float32)).astype(jnp.bfloat16)


def dot_rows(a, b):
    dims = (((1,), (1,)), ((), ()))
    mul = lambda p, q: lax.dot_general(p, q, dims, preferred_element_type=jnp.float32)
    return mul(a[0], b[0]) + (mul(a[0], b[1]) + mul(a[1], b[0]))


def dot_plain(a, b):
    dims = (((1,), (0,)), ((), ()))
    mul = lambda p, q: lax.dot_general(p, q, dims, preferred_element_type=jnp.float32)
    return mul(a[0], b[0]) + (mul(a[0], b[1]) + mul(a[1], b[0]))


def z_partners():
    runs = SIZES[2]
    ahead = [((1, r), (2, r)) for r in range(runs)]
    ahead += [((3, r), (0, (r + 1) % runs)) for r in range(runs)]
    flat = lambda at: at[0] * runs + at[1]
    return [(flat(p), flat(q)) for p, q in ahead] + [(flat(q), flat(p)) for p, q in ahead]


def block_copies(order_ref, feats_ref, out_ref, sems, first, brow, column):
    half = feats_ref.shape[0] // 2
    width = out_ref.shape[2]
    own = pl.ds(pl.multiple_of(lax.axis_index("c") * half, half), half)
    return [
        pltpu.make_async_copy(
            feats_ref.at[own, pl.ds(pl.multiple_of(order_ref[x * 2 + column, brow] * width, width), width)],
            out_ref.at[x, pl.ds(first, half), :],
            sems.at[x],
        )
        for x in range(out_ref.shape[0])
    ]


def lend_kernel(order_ref, feats_ref, out_ref, sems):
    zl = lax.axis_index("zl")
    runs = lax.axis_size("zh")
    turn = jnp.where(zl == 3, 1, jnp.where(zl == 0, runs - 1, 0))
    brow = lax.rem(lax.axis_index("zh") + turn, runs) * lax.axis_size("y") + lax.axis_index("y")
    copies = block_copies(order_ref, feats_ref, out_ref, sems, 0, brow, 1 - zl // 2)
    for copy in copies:
        copy.start()
    for copy in copies:
        copy.wait()


def mask_kernel(counts_ref, grads_ref, out_ref):
    rows = lax.broadcasted_iota(jnp.int32, grads_ref.shape, 0)
    count = counts_ref[lax.axis_index("x") * lax.axis_size("zl") + lax.axis_index("zl")]
    masked = jnp.where(rows < count, grads_ref[...].astype(jnp.float32), 0.0)
    out_ref[...] = masked.astype(jnp.bfloat16)


def grads_copies(grads_ref, out_ref, sems, first):
    half = grads_ref.shape[0] // 2
    width = grads_ref.shape[1]
    return [
        pltpu.make_async_copy(
            grads_ref.at[pl.ds(half * part, half), :],
            out_ref.at[x, pl.ds(first, half), pl.ds(width * part, width)],
            sems.at[x, part],
        )
        for x in range(out_ref.shape[0])
        for part in range(2)
    ]


def own_kernel(order_ref, feats_ref, grads_ref, out_ref, sems, grads_sems):
    half = feats_ref.shape[0] // 2
    brow = lax.axis_index("zh") * lax.axis_size("y") + lax.axis_index("y")
    copies = block_copies(order_ref, feats_ref, out_ref, sems, 0, brow, lax.axis_index("zl") // 2)
    copies += grads_copies(grads_ref, out_ref, grads_sems, 2 * half)
    for copy in copies:
        copy.start()
    for copy in copies:
        copy.wait()


def lent_kernel(feats_ref, grads_ref, filled_ref, out_ref, sems, grads_sems):
    half = feats_ref.shape[1]
    copies = [
        pltpu.make_async_copy(feats_ref.at[x], out_ref.at[x, pl.ds(half, half), :], sems.at[x])
        for x in range(out_ref.shape[0])
    ]
    copies += grads_copies(grads_ref, out_ref, grads_sems, 3 * half)
    for copy in copies:
        copy.start()
    for copy in copies:
        copy.wait()


def lane_sums(value):
    squares = jnp.sum(value * value, axis=0, keepdims=True)
    return squares[:, :128] + squares[:, 128:]


def moment_kernel(
    own_ref,
    moment_ref,
    second_ref,
    mine_ref,
    other_ref,
    new_moment_ref,
    new_second_ref,
    sum_ref,
    inner_ref,
    high_ref,
    low_ref,
    left_ref,
):
    half = own_ref.shape[0]
    quarter = half // 2
    side = lax.axis_index("c")
    part = lax.rem(lax.axis_index("zl"), 2)
    place = lambda i, n: pl.ds(pl.multiple_of(i * n, n), n)
    tile = own_ref[:, place(part, half)]
    new_moment = 0.9 * moment_ref[...] + 0.1 * tile
    new_second = 0.95 * second_ref[...] + 0.05 * tile * tile
    new_moment_ref[...] = new_moment
    new_second_ref[...] = new_second
    sum_ref[...] = lane_sums(new_moment / (jnp.sqrt(new_second) + 1e-08))
    left_ref[place(part, quarter), :] = mine_ref[...]
    left_ref[place(1 - part, quarter), :] = other_ref[...]
    inner_ref[...] = dot_plain(split(left_ref[:, place(side, half)]), split(own_ref[...]))
    high_ref[...], low_ref[...] = split(left_ref[:, place(1 - side, half)])


def step_kernel(
    inner_ref,
    other_ref,
    left_high_ref,
    left_low_ref,
    right_mine_ref,
    right_other_ref,
    sum_ref,
    precond_ref,
    sums_ref,
    right_ref,
):
    quarter = right_mine_ref.shape[0]
    side = lax.axis_index("c")
    place = lambda i, n: pl.ds(pl.multiple_of(i * n, n), n)
    right_ref[place(side, quarter), :] = right_mine_ref[...]
    right_ref[place(1 - side, quarter), :] = right_other_ref[...]
    left = (left_high_ref[...], left_low_ref[...])
    inner = inner_ref[...] + dot_plain(left, split(other_ref[...]))
    precond = dot_rows(split(inner), split(right_ref[...]))
    precond_ref[...] = precond
    sums = jnp.concatenate([sum_ref[...], lane_sums(precond)], 0)
    sums_ref[...] = jnp.broadcast_to(sums[None], sums_ref.shape)


def scale_kernel(sums_ref, precond_ref, out_ref):
    total = jnp.sum(sums_ref[...], axis=0)
    across = lambda v: jnp.sum(jnp.sum(v, axis=1, keepdims=True), axis=0, keepdims=True)
    scale = jnp.sqrt(across(total[0:1]) / (across(total[1:2]) + 1e-06))
    out_ref[...] = scale * precond_ref[...]


def call(kernel, out_shape, in_specs, out_specs, scratch_shapes=(), aliases=None):
    return pl.pallas_call(
        kernel,
        out_shape=out_shape,
        in_specs=in_specs,
        out_specs=out_specs,
        scratch_shapes=scratch_shapes,
        input_output_aliases=aliases or {},
        compiler_params=pltpu.CompilerParams(vmem_limit_bytes=VMEM_LIMIT),
    )


VM = pl.BlockSpec(memory_space=pltpu.VMEM)
SM = pl.BlockSpec(memory_space=pltpu.SMEM)
ANY = pl.BlockSpec(memory_space=pl.ANY)


def body(
    features,
    out_grads,
    token_counts,
    owner_order,
    moment,
    second,
    left_stat,
    right_stat,
    left_root,
    right_root,
):
    f32 = jnp.float32
    tok_rows = features.shape[0]
    block_size = left_stat.shape[-1]
    half_size = block_size // 2
    quarter = block_size // 4
    side_bit = lax.axis_index("c")
    part_bit = lax.axis_index("zl") % 2
    precise = lax.Precision.HIGH
    token_total = jnp.sum(token_counts).astype(f32)
    left_mine = left_root[0, 0]
    right_mine = right_root[0, 0]

    half_rows = tok_rows // 2
    lines = lax.axis_size("x")
    order = owner_order.T
    lent = call(
        lend_kernel,
        jax.ShapeDtypeStruct((lines, half_rows, block_size), jnp.bfloat16),
        [SM, ANY],
        VM,
        [pltpu.SemaphoreType.DMA((lines,))],
    )(order, features)
    lent = lax.ppermute(lent, ("zl", "zh"), z_partners())
    masked = jax.ShapeDtypeStruct(out_grads.shape, jnp.bfloat16)
    grads = call(mask_kernel, masked, [SM, VM], VM)(token_counts, out_grads)
    lent_grads = lax.ppermute(grads, "zl", [(i, 3 - i) for i in range(4)])
    packed = jax.ShapeDtypeStruct((lines, 4 * half_rows, block_size), jnp.bfloat16)
    sems = [pltpu.SemaphoreType.DMA((lines,)), pltpu.SemaphoreType.DMA((lines, 2))]
    filled = call(own_kernel, packed, [SM, ANY, VM], ANY, sems)(order, features, grads)
    outgoing = call(lent_kernel, packed, [VM, VM, ANY], ANY, sems, {2: 0})(
        lent, lent_grads, filled
    )
    left_other = partner(left_mine, "zl")
    right_other = partner(right_mine, "c")
    arrived = lax.all_to_all(outgoing, "x", split_axis=0, concat_axis=0, tiled=True)
    arrived, left_other, right_other = lax.optimization_barrier(
        (arrived, left_other, right_other)
    )
    feats_own = arrived[:, :tok_rows].reshape(-1, block_size)
    feats_other = partner(feats_own, "c")
    grads_low = arrived[:, tok_rows:, :half_size].reshape(-1, half_size)
    grads_high = arrived[:, tok_rows:, half_size:].reshape(-1, half_size)
    own_first = side_bit == 0
    grads_own = jnp.where(own_first, grads_low, grads_high)
    grads_other = jnp.where(own_first, grads_high, grads_low)
    partial = jnp.dot(grads_own.T, feats_own, preferred_element_type=f32) + jnp.dot(
        grads_other.T, feats_other, preferred_element_type=f32
    )
    own_half = (partial + partner(partial, "zl")) / token_total
    other_half = partner(own_half, "c")

    tile = jax.ShapeDtypeStruct((half_size, half_size), f32)
    piece = jax.ShapeDtypeStruct((half_size, half_size), jnp.bfloat16)
    rows = jax.ShapeDtypeStruct((half_size, block_size), f32)
    new_moment, new_second, direction_sum, inner, left_high, left_low = call(
        moment_kernel,
        (tile, tile, jax.ShapeDtypeStruct((1, 128), f32), rows, piece, piece),
        [VM] * 5,
        (VM,) * 6,
        [pltpu.VMEM(rows.shape, f32)],
    )(own_half, moment, second, left_mine, left_other)
    near = ("x", "y", "c")
    line = ("zl", "zh")
    precond, sums = call(
        step_kernel,
        (tile, jax.ShapeDtypeStruct((lax.axis_size(near), 2, 128), f32)),
        [VM] * 7,
        (VM,) * 2,
        [pltpu.VMEM(rows.shape, f32)],
    )(inner, other_half, left_high, left_low, right_mine, right_other, direction_sum)
    sums = lax.all_to_all(sums, near, split_axis=0, concat_axis=0, tiled=True)
    sums = jnp.broadcast_to(jnp.sum(sums, 0), (lax.axis_size(line), 2, 128))
    sums = lax.all_to_all(sums, line, split_axis=0, concat_axis=0, tiled=True)
    update = call(scale_kernel, tile, [VM, VM], VM)(sums, precond)

    whole_block = jnp.where(
        own_first,
        jnp.concatenate([own_half, other_half], 0),
        jnp.concatenate([other_half, own_half], 0),
    )
    left_rows = lax.dynamic_slice_in_dim(own_half, part_bit * quarter, quarter, 0)
    right_cols = lax.dynamic_slice_in_dim(
        whole_block, part_bit * half_size + side_bit * quarter, quarter, 1
    )
    next_left = 0.95 * left_stat[0, 0] + 0.05 * (
        jnp.dot(left_rows, whole_block.T, precision=precise) / block_size
    )
    next_right = 0.95 * right_stat[0, 0] + 0.05 * (
        jnp.dot(right_cols.T, whole_block, precision=precise) / block_size
    )
    return (update, new_moment, new_second, next_left[None, None], next_right[None, None])


def solution(mesh):
    fine = Mesh(mesh.devices.reshape(SIZES), DP + SHARD)
    return jax.shard_map(
        body,
        mesh=fine,
        in_specs=(
            P(DP, None),
            P(DP, SHARD),
            P(),
            P(),
            P(SHARD, DP),
            P(SHARD, DP),
            P(SHARD, DP, None, None),
            P(SHARD, DP, None, None),
            P(SHARD, DP, None, None),
            P(SHARD, DP, None, None),
        ),
        out_specs=(
            P(SHARD, DP),
            P(SHARD, DP),
            P(SHARD, DP),
            P(SHARD, DP, None, None),
            P(SHARD, DP, None, None),
        ),
        check_vma=False,
    )
```

profile of v0, /device:TPU:1, one launch (start us, length us, event | category | flops | bytes accessed | tf_op | source)
XLA Modules:
  0.0 113.5 jit_solution(5508411374117079642)
XLA Ops:
  0.6 1.2 %copy-done = bf16[128,4096]{1,0:T(8,128)(2,1)S(1)} copy-done((bf16[128,4096]{1,0:T(8,128)(2,1)S(1)}, bf16[128,4096]{1,0:T(8,128)(2,1)}, u32[]{:S(2)}) %copy-start) | copy-done | bytes 1048600
  1.9 0.7 copy-done.7
  2.6 0.7 shard_map.137
  3.3 18.8 %collective-permute-start = (bf16[4,64,512]{2,1,0:T(8,128)(2,1)S(1)}, bf16[4,64,512]{2,1,0:T(8,128)(2,1)S(1)}, u32[]{:S(2)}, u32[]{:S(2)}) collective-permute-start(bf16[4,64,512]{2,1,0:T(8,128)(2,1)S(1)} %shard_map.137), channel_id=1, source_target_pairs={{64,128},{80,144},{96,160},{112,176},{192,16},{208,32},{224,48},{2... | collective-permute-start | bytes 786440 | tf_op jit(solution)/shard_map/ppermute | solution.py:233
  22.1 0.6 shard_map.138.grads_ref
  22.7 1.9 %collective-permute-start.1 = (bf16[128,256]{1,0:T(8,128)(2,1)S(1)}, bf16[128,256]{1,0:T(8,128)(2,1)S(1)}, u32[]{:S(2)}, u32[]{:S(2)}) collective-permute-start(bf16[128,256]{1,0:T(8,128)(2,1)S(1)} %shard_map.138.grads_ref), channel_id=1, source_target_pairs={{0,192},{64,128},{128,64},{192,0},{1,193},{65,129},{129,65},{193,1... | collective-permute-start | bytes 196616 | tf_op jit(solution)/shard_map/ppermute | solution.py:236
  24.6 1.5 %shard_map.139.filled_ref = bf16[4,256,512]{2,1,0:T(8,128)(2,1)} custom-call(s32[8,32]{1,0:T(8,128)S(1)} %bitcast.26, bf16[128,4096]{1,0:T(8,128)(2,1)S(1)} %copy-done.1, bf16[128,256]{1,0:T(8,128)(2,1)S(1)} %shard_map.138.grads_ref), custom_call_target="tpu_custom_call" | custom-call | tf_op jit(solution)/shard_map/pallas_call | solution.py:239
  26.1 3.3 %collective-permute-done.1.grads_ref = bf16[128,256]{1,0:T(8,128)(2,1)S(1)} collective-permute-done((bf16[128,256]{1,0:T(8,128)(2,1)S(1)}, bf16[128,256]{1,0:T(8,128)(2,1)S(1)}, u32[]{:S(2)}, u32[]{:S(2)}) %collective-permute-start.1) | collective-permute-done | bytes 65568 | tf_op jit(solution)/shard_map/ppermute | solution.py:236
  29.5 0.9 shard_map.140
  30.4 4.2 %all-to-all-start = ((bf16[4,256,512]{2,1,0:T(8,128)(2,1)}), bf16[4,256,512]{2,1,0:T(8,128)(2,1)S(1)}, u32[]{:S(2)}, u32[]{:S(2)}) async-start(bf16[4,256,512]{2,1,0:T(8,128)(2,1)} %shard_map.140), calls=%async_computation | async-start | bytes 2097152 | tf_op jit(solution)/shard_map/all_to_all | solution.py:245
  34.6 1.9 %collective-permute-start.2 = (f32[128,512]{1,0:T(8,128)S(1)}, f32[128,512]{1,0:T(8,128)S(1)}, u32[]{:S(2)}, u32[]{:S(2)}) collective-permute-start(f32[128,512]{1,0:T(8,128)S(1)} %bitcast.21), channel_id=1, source_target_pairs={{0,64},{64,0},{128,192},{192,128},{1,65},{65,1},{129,193},{193,129... | collective-permute-start | bytes 786440 | tf_op jit(solution)/shard_map/ppermute | solution.py:15
  36.5 4.3 %collective-permute-start.3 = (f32[128,512]{1,0:T(8,128)S(1)}, f32[128,512]{1,0:T(8,128)S(1)}, u32[]{:S(2)}, u32[]{:S(2)}) collective-permute-start(f32[128,512]{1,0:T(8,128)S(1)} %bitcast.23), channel_id=1, source_target_pairs={{0,1},{1,0},{2,3},{3,2},{4,5},{5,4},{6,7},{7,6},{8,9},{9,8},{10,11... | collective-permute-start | bytes 786440 | tf_op jit(solution)/shard_map/ppermute | solution.py:15
  40.8 1.2 %collective-permute-done.2.other_ref = f32[128,512]{1,0:T(8,128)S(1)} collective-permute-done((f32[128,512]{1,0:T(8,128)S(1)}, f32[128,512]{1,0:T(8,128)S(1)}, u32[]{:S(2)}, u32[]{:S(2)}) %collective-permute-start.2) | collective-permute-done | bytes 262176 | tf_op jit(solution)/shard_map/ppermute | solution.py:15
  42.0 5.0 %all-to-all-done = bf16[4,256,512]{2,1,0:T(8,128)(2,1)S(1)} async-done(((bf16[4,256,512]{2,1,0:T(8,128)(2,1)}), bf16[4,256,512]{2,1,0:T(8,128)(2,1)S(1)}, u32[]{:S(2)}, u32[]{:S(2)}) %all-to-all-start) | async-done | bytes 1048608 | tf_op jit(solution)/shard_map/all_to_all | solution.py:245
  47.0 0.8 slice.11
  47.9 5.5 %collective-permute-start.4 = (bf16[512,512]{1,0:T(8,128)(2,1)}, bf16[512,512]{1,0:T(8,128)(2,1)S(1)}, u32[]{:S(2)}, u32[]{:S(2)}) collective-permute-start(bf16[512,512]{1,0:T(8,128)(2,1)} %bitcast.5), channel_id=1, source_target_pairs={{0,1},{1,0},{2,3},{3,2},{4,5},{5,4},{6,7},{7,6},{8,9},{9,8},{10,11... | collective-permute-start | bytes 1572872 | tf_op jit(solution)/shard_map/ppermute | solution.py:15
  53.4 1.7 %collective-permute-done.4 = bf16[512,512]{1,0:T(8,128)(2,1)S(1)} collective-permute-done((bf16[512,512]{1,0:T(8,128)(2,1)}, bf16[512,512]{1,0:T(8,128)(2,1)S(1)}, u32[]{:S(2)}, u32[]{:S(2)}) %collective-permute-start.4) | collective-permute-done | bytes 524320 | tf_op jit(solution)/shard_map/ppermute | solution.py:15
  55.8 1.9 %collective-permute-start.5 = (f32[256,512]{1,0:T(8,128)S(1)}, f32[256,512]{1,0:T(8,128)S(1)}, u32[]{:S(2)}, u32[]{:S(2)}) collective-permute-start(f32[256,512]{1,0:T(8,128)S(1)} %fusion), channel_id=1, source_target_pairs={{0,64},{64,0},{128,192},{192,128},{1,65},{65,1},{129,193},{193,129... | collective-permute-start | bytes 1572872 | tf_op jit(solution)/shard_map/ppermute | solution.py:15
  57.7 0.6 reduce_sum.18
  59.0 11.8 %collective-permute-done.5 = f32[256,512]{1,0:T(8,128)S(1)} collective-permute-done((f32[256,512]{1,0:T(8,128)S(1)}, f32[256,512]{1,0:T(8,128)S(1)}, u32[]{:S(2)}, u32[]{:S(2)}) %collective-permute-start.5) | collective-permute-done | bytes 524320 | tf_op jit(solution)/shard_map/ppermute | solution.py:15
  70.9 3.1 %collective-permute-start.6 = (f32[256,512]{1,0:T(8,128)S(1)}, f32[256,512]{1,0:T(8,128)S(1)}, u32[]{:S(2)}, u32[]{:S(2)}) collective-permute-start(f32[256,512]{1,0:T(8,128)S(1)} %add_divide_fusion.own_ref), channel_id=1, source_target_pairs={{0,1},{1,0},{2,3},{3,2},{4,5},{5,4},{6,7},{7,6},{8,9},{9,8},{10,11... | collective-permute-start | bytes 1572872 | tf_op jit(solution)/shard_map/ppermute | solution.py:15
  74.0 1.2 %shard_map.141 = (f32[256,256]{1,0:T(8,128)}, f32[256,256]{1,0:T(8,128)}, f32[1,128]{1,0:T(1,128)S(1)}, f32[256,512]{1,0:T(8,128)S(1)}, bf16[256,256]{1,0:T(8,128)(2,1)S(1)}, /*index=5*/bf16[256,256]{1,0:T(8,128)(2,1)S(1)}) custom-call(f32[256,512]{1,0:T(8,128)S(1)} %add_divide_fusion.own_ref, f32[256,256]{1,0:T(8,128)S(1)} %copy-done.2, ...), custom_call_target="tpu_custom_call" | custom-call | tf_op jit(solution)/shard_map/pallas_call | solution.py:265
  75.5 1.6 %shard_map.142 = (f32[256,256]{1,0:T(8,128)S(1)}, f32[64,2,128]{2,1,0:T(2,128)}) custom-call(f32[256,512]{1,0:T(8,128)S(1)} %get-tuple-element.18.inner_ref, f32[256,512]{1,0:T(8,128)S(1)} %collective-permute-done.6.other_ref, bf16[256,256]{1,0:T(8,128)(2,1)S(1)} %get-tuple-element.19.left_high_ref, bf16[256,256]{1,0:T(8,128)(2,1)S(1)} %get-tuple-element.20.left_low_ref, ...), custom_call_target="tpu_custom_call" | custom-call | tf_op jit(solution)/shard_map/pallas_call | solution.py:274
  77.1 8.6 %all-to-all-start.1 = ((f32[64,2,128]{2,1,0:T(2,128)}), f32[64,2,128]{2,1,0:T(2,128)S(1)}, u32[]{:S(2)}, u32[]{:S(2)}) async-start(f32[64,2,128]{2,1,0:T(2,128)} %get-tuple-element.23), calls=%async_computation.1 | async-start | bytes 131072 | tf_op jit(solution)/shard_map/all_to_all | solution.py:281
  85.9 0.8 copy-done.10
  86.7 1.4 %fusion.4 = f32[1,1,128,512]{3,2,1,0:T(8,128)} fusion(f32[512,512]{1,0:T(8,128)S(1)} %maximum_select_fusion, f32[256,512]{1,0:T(8,128)S(1)} %add_divide_fusion.own_ref, s32[]{:T(128)S(6)} %select_n.42, f32[1,1,128,512]{3,2,1,0:T(8,128)S(1)} %copy-done.10), kind=kOutput, calls=%fused_computation.7 | convolution fusion | flops 201523200 | bytes 1835012 | tf_op jit(solution)/shard_map/dot_general | solution.py:296
  88.1 7.5 %all-to-all-done.1 = f32[64,2,128]{2,1,0:T(2,128)S(1)} async-done(((f32[64,2,128]{2,1,0:T(2,128)}), f32[64,2,128]{2,1,0:T(2,128)S(1)}, u32[]{:S(2)}, u32[]{:S(2)}) %all-to-all-start.1) | async-done | bytes 65568 | tf_op jit(solution)/shard_map/all_to_all | solution.py:281
  95.6 0.6 broadcast_in_dim.9
  96.2 5.1 %all-to-all-start.2 = ((f32[16,2,128]{2,1,0:T(2,128)}), f32[16,2,128]{2,1,0:T(2,128)S(1)}, u32[]{:S(2)}, u32[]{:S(2)}) async-start(f32[16,2,128]{2,1,0:T(2,128)} %broadcast_in_dim.9), calls=%async_computation.2 | async-start | bytes 32768 | tf_op jit(solution)/shard_map/all_to_all | solution.py:283
  101.3 1.2 %fusion.2 = f32[1,1,128,512]{3,2,1,0:T(8,128)} fusion(f32[512,512]{1,0:T(8,128)S(1)} %maximum_select_fusion, s32[]{:T(128)S(6)} %select_n.45, f32[1,1,128,512]{3,2,1,0:T(8,128)S(1)} %copy-done.11), kind=kOutput, calls=%fused_computation.4 | convolution fusion | flops 201523200 | bytes 1835012 | tf_op jit(solution)/shard_map/dot_general | solution.py:299
  102.5 10.1 %all-to-all-done.2.sums_ref = f32[16,2,128]{2,1,0:T(2,128)S(1)} async-done(((f32[16,2,128]{2,1,0:T(2,128)}), f32[16,2,128]{2,1,0:T(2,128)S(1)}, u32[]{:S(2)}, u32[]{:S(2)}) %all-to-all-start.2) | async-done | bytes 16416 | tf_op jit(solution)/shard_map/all_to_all | solution.py:283
  112.6 0.9 shard_map.143
  (30 shorter events, 1.3 us)
Async XLA Ops:
  0.6 1.2 %copy-start = (bf16[128,4096]{1,0:T(8,128)(2,1)S(1)}, bf16[128,4096]{1,0:T(8,128)(2,1)}, u32[]{:S(2)}) copy-start(bf16[128,4096]{1,0:T(8,128)(2,1)} %feats_ref.3) | copy-start | bytes 3145732
  1.9 0.7 copy-start.7
  2.5 19.5 %copy-start.6 = (bf16[128,256]{1,0:T(8,128)(2,1)S(1)}, bf16[128,256]{1,0:T(8,128)(2,1)}, u32[]{:S(2)}) copy-start(bf16[128,256]{1,0:T(8,128)(2,1)} %grads_ref.1) | copy-start | bytes 196612
  2.5 19.5 %copy-start.9 = (s32[16]{0:T(128)S(1)}, s32[16]{0:T(128)}, u32[]{:S(2)}) copy-start(s32[16]{0:T(128)} %counts_ref.1) | copy-start | bytes 196
  2.5 22.0 %copy-start.1 = (bf16[128,4096]{1,0:T(8,128)(2,1)S(1)}, bf16[128,4096]{1,0:T(8,128)(2,1)}, u32[]{:S(2)}) copy-start(bf16[128,4096]{1,0:T(8,128)(2,1)} %feats_ref.3) | copy-start | bytes 3145732
  3.3 21.3 %copy-start.8 = (s32[32,8]{0,1:T(8,128)S(1)}, s32[32,8]{0,1:T(8,128)}, u32[]{:S(2)}) copy-start(s32[32,8]{0,1:T(8,128)} %param.13) | copy-start | bytes 3076
  3.3 26.2 %collective-permute-start = (bf16[4,64,512]{2,1,0:T(8,128)(2,1)S(1)}, bf16[4,64,512]{2,1,0:T(8,128)(2,1)S(1)}, u32[]{:S(2)}, u32[]{:S(2)}) collective-permute-start(bf16[4,64,512]{2,1,0:T(8,128)(2,1)S(1)} %shard_map.137), channel_id=1, source_target_pairs={{64,128},{80,144},{96,160},{112,176},{192,16},{208,32},{224,48},{2... | collective-permute-start | bytes 786440 | tf_op jit(solution)/shard_map/ppermute | solution.py:233
  22.7 6.8 %collective-permute-start.1 = (bf16[128,256]{1,0:T(8,128)(2,1)S(1)}, bf16[128,256]{1,0:T(8,128)(2,1)S(1)}, u32[]{:S(2)}, u32[]{:S(2)}) collective-permute-start(bf16[128,256]{1,0:T(8,128)(2,1)S(1)} %shard_map.138.grads_ref), channel_id=1, source_target_pairs={{0,192},{64,128},{128,64},{192,0},{1,193},{65,129},{129,65},{193,1... | collective-permute-start | bytes 196616 | tf_op jit(solution)/shard_map/ppermute | solution.py:236
  30.4 4.2 %copy-start.4 = (f32[1,1,128,512]{3,2,1,0:T(8,128)S(1)}, f32[1,1,128,512]{3,2,1,0:T(8,128)}, u32[]{:S(2)}) copy-start(f32[1,1,128,512]{3,2,1,0:T(8,128)} %param.18) | copy-start | bytes 786436
  30.4 6.1 %copy-start.5 = (f32[1,1,128,512]{3,2,1,0:T(8,128)S(1)}, f32[1,1,128,512]{3,2,1,0:T(8,128)}, u32[]{:S(2)}) copy-start(f32[1,1,128,512]{3,2,1,0:T(8,128)} %param.19) | copy-start | bytes 786436
  30.4 16.6 %all-to-all-start = ((bf16[4,256,512]{2,1,0:T(8,128)(2,1)}), bf16[4,256,512]{2,1,0:T(8,128)(2,1)S(1)}, u32[]{:S(2)}, u32[]{:S(2)}) async-start(bf16[4,256,512]{2,1,0:T(8,128)(2,1)} %shard_map.140), calls=%async_computation | async-start | bytes 2097152 | tf_op jit(solution)/shard_map/all_to_all | solution.py:245
  34.6 7.4 %collective-permute-start.2 = (f32[128,512]{1,0:T(8,128)S(1)}, f32[128,512]{1,0:T(8,128)S(1)}, u32[]{:S(2)}, u32[]{:S(2)}) collective-permute-start(f32[128,512]{1,0:T(8,128)S(1)} %bitcast.21), channel_id=1, source_target_pairs={{0,64},{64,0},{128,192},{192,128},{1,65},{65,1},{129,193},{193,129... | collective-permute-start | bytes 786440 | tf_op jit(solution)/shard_map/ppermute | solution.py:15
  36.5 5.5 %collective-permute-start.3 = (f32[128,512]{1,0:T(8,128)S(1)}, f32[128,512]{1,0:T(8,128)S(1)}, u32[]{:S(2)}, u32[]{:S(2)}) collective-permute-start(f32[128,512]{1,0:T(8,128)S(1)} %bitcast.23), channel_id=1, source_target_pairs={{0,1},{1,0},{2,3},{3,2},{4,5},{5,4},{6,7},{7,6},{8,9},{9,8},{10,11... | collective-permute-start | bytes 786440 | tf_op jit(solution)/shard_map/ppermute | solution.py:15
  47.9 7.2 %collective-permute-start.4 = (bf16[512,512]{1,0:T(8,128)(2,1)}, bf16[512,512]{1,0:T(8,128)(2,1)S(1)}, u32[]{:S(2)}, u32[]{:S(2)}) collective-permute-start(bf16[512,512]{1,0:T(8,128)(2,1)} %bitcast.5), channel_id=1, source_target_pairs={{0,1},{1,0},{2,3},{3,2},{4,5},{5,4},{6,7},{7,6},{8,9},{9,8},{10,11... | collective-permute-start | bytes 1572872 | tf_op jit(solution)/shard_map/ppermute | solution.py:15
  55.8 15.0 %collective-permute-start.5 = (f32[256,512]{1,0:T(8,128)S(1)}, f32[256,512]{1,0:T(8,128)S(1)}, u32[]{:S(2)}, u32[]{:S(2)}) collective-permute-start(f32[256,512]{1,0:T(8,128)S(1)} %fusion), channel_id=1, source_target_pairs={{0,64},{64,0},{128,192},{192,128},{1,65},{65,1},{129,193},{193,129... | collective-permute-start | bytes 1572872 | tf_op jit(solution)/shard_map/ppermute | solution.py:15
  59.0 15.1 %copy-start.2 = (f32[256,256]{1,0:T(8,128)S(1)}, f32[256,256]{1,0:T(8,128)}, u32[]{:S(2)}) copy-start(f32[256,256]{1,0:T(8,128)} %moment_ref.1) | copy-start | bytes 786436
  59.0 15.1 %copy-start.3 = (f32[256,256]{1,0:T(8,128)S(1)}, f32[256,256]{1,0:T(8,128)}, u32[]{:S(2)}) copy-start(f32[256,256]{1,0:T(8,128)} %second_ref.1) | copy-start | bytes 786436
  70.9 4.6 %collective-permute-start.6 = (f32[256,512]{1,0:T(8,128)S(1)}, f32[256,512]{1,0:T(8,128)S(1)}, u32[]{:S(2)}, u32[]{:S(2)}) collective-permute-start(f32[256,512]{1,0:T(8,128)S(1)} %add_divide_fusion.own_ref), channel_id=1, source_target_pairs={{0,1},{1,0},{2,3},{3,2},{4,5},{5,4},{6,7},{7,6},{8,9},{9,8},{10,11... | collective-permute-start | bytes 1572872 | tf_op jit(solution)/shard_map/ppermute | solution.py:15
  77.1 18.4 %all-to-all-start.1 = ((f32[64,2,128]{2,1,0:T(2,128)}), f32[64,2,128]{2,1,0:T(2,128)S(1)}, u32[]{:S(2)}, u32[]{:S(2)}) async-start(f32[64,2,128]{2,1,0:T(2,128)} %get-tuple-element.23), calls=%async_computation.1 | async-start | bytes 131072 | tf_op jit(solution)/shard_map/all_to_all | solution.py:281
  85.8 1.0 copy-start.10
  86.7 14.6 %copy-start.11 = (f32[1,1,128,512]{3,2,1,0:T(8,128)S(1)}, f32[1,1,128,512]{3,2,1,0:T(8,128)}, u32[]{:S(2)}) copy-start(f32[1,1,128,512]{3,2,1,0:T(8,128)} %param.17) | copy-start | bytes 786436
  96.2 16.4 %all-to-all-start.2 = ((f32[16,2,128]{2,1,0:T(2,128)}), f32[16,2,128]{2,1,0:T(2,128)S(1)}, u32[]{:S(2)}, u32[]{:S(2)}) async-start(f32[16,2,128]{2,1,0:T(2,128)} %broadcast_in_dim.9), calls=%async_computation.2 | async-start | bytes 32768 | tf_op jit(solution)/shard_map/all_to_all | solution.py:283
where the time goes:
time: 114 us; the launch traced here: 113 us
  starting transfers between devices  55.3 us (49%)
  waiting for transfers between devices  40.8 us (36%)
  Pallas kernels  7.39 us (6%)
  local copies, waits for them, and re-layouts  4.22 us (4%)
  matrix products  3.22 us (3%)
  between operations  1.58 us (1%)
    ppermute x1, starting transfers between devices, body(): lent = lax.ppermute(lent, ('zl', 'zh'), z_partners())  18.8 us
    ppermute x5, starting transfers between devices, partner(): lax.ppermute(value, axis, [(i, i ^ 1) for i in range(lax.axis_size(axis))])  16.7 us
    ppermute x5, waiting for transfers between devices, partner(): lax.ppermute(value, axis, [(i, i ^ 1) for i in range(lax.axis_size(axis))])  14.9 us
    all_to_all x1, waiting for transfers between devices, body(): sums = lax.all_to_all(sums, line, split_axis=0, concat_axis=0, tiled=True)  10.1 us
    all_to_all x1, starting transfers between devices, body(): sums = lax.all_to_all(sums, near, split_axis=0, concat_axis=0, tiled=True)  8.63 us
    all_to_all x1, waiting for transfers between devices, body(): sums = lax.all_to_all(sums, near, split_axis=0, concat_axis=0, tiled=True)  7.45 us
    all_to_all x1, starting transfers between devices, body(): sums = lax.all_to_all(sums, line, split_axis=0, concat_axis=0, tiled=True)  5.09 us
    all_to_all x1, waiting for transfers between devices, body(): lax.all_to_all(outgoing, 'x', split_axis=0, concat_axis=0, tiled=True)  5.04 us
  transfers between devices with their start and end apart: 10, of which 8 were waited for; matrix products, arithmetic and copies ran while one was open for 3% of the time, Pallas kernels for 3%

commit v1 on v0

--- a/solution.py
+++ b/solution.py
@@ -279,16 +279,17 @@
         [pltpu.VMEM(rows.shape, f32)],
     )(inner, other_half, left_high, left_low, right_mine, right_other, direction_sum)
     sums = lax.all_to_all(sums, near, split_axis=0, concat_axis=0, tiled=True)
+    sums, own_rows, other_rows = lax.optimization_barrier((sums, own_half, other_half))
     sums = jnp.broadcast_to(jnp.sum(sums, 0), (lax.axis_size(line), 2, 128))
     sums = lax.all_to_all(sums, line, split_axis=0, concat_axis=0, tiled=True)
     update = call(scale_kernel, tile, [VM, VM], VM)(sums, precond)
 
     whole_block = jnp.where(
         own_first,
-        jnp.concatenate([own_half, other_half], 0),
-        jnp.concatenate([other_half, own_half], 0),
-    )
-    left_rows = lax.dynamic_slice_in_dim(own_half, part_bit * quarter, quarter, 0)
+        jnp.concatenate([own_rows, other_rows], 0),
+        jnp.concatenate([other_rows, own_rows], 0),
+    )
+    left_rows = lax.dynamic_slice_in_dim(own_rows, part_bit * quarter, quarter, 0)
     right_cols = lax.dynamic_slice_in_dim(
         whole_block, part_bit * half_size + side_bit * quarter, quarter, 1
     )

time: 114 us -> 114 us (level)
    all_to_all x1, waiting for transfers between devices: 10.1 us -> 7.72 us  [body(): sums = lax.all_to_all(sums, line, split_axis=0, concat_axis=0, tiled=True)]
    all_to_all x1, waiting for transfers between devices: 7.45 us -> 9.76 us  [body(): sums = lax.all_to_all(sums, near, split_axis=0, concat_axis=0, tiled=True)]
where the time goes in v1:
time: 114 us; the launch traced here: 113 us
  starting transfers between devices  55.3 us (49%)
  waiting for transfers between devices  40.8 us (36%)
  Pallas kernels  7.4 us (6%)
  local copies, waits for them, and re-layouts  4.24 us (4%)
  matrix products  3.25 us (3%)
  between operations  1.57 us (1%)
    ppermute x1, starting transfers between devices, body(): lent = lax.ppermute(lent, ('zl', 'zh'), z_partners())  18.8 us
    ppermute x5, starting transfers between devices, partner(): lax.ppermute(value, axis, [(i, i ^ 1) for i in range(lax.axis_size(axis))])  16.7 us
    ppermute x5, waiting for transfers between devices, partner(): lax.ppermute(value, axis, [(i, i ^ 1) for i in range(lax.axis_size(axis))])  14.9 us
    all_to_all x1, waiting for transfers between devices, body(): sums = lax.all_to_all(sums, near, split_axis=0, concat_axis=0, tiled=True)  9.76 us
    all_to_all x1, starting transfers between devices, body(): sums = lax.all_to_all(sums, near, split_axis=0, concat_axis=0, tiled=True)  8.63 us
    all_to_all x1, waiting for transfers between devices, body(): sums = lax.all_to_all(sums, line, split_axis=0, concat_axis=0, tiled=True)  7.72 us
    all_to_all x1, starting transfers between devices, body(): sums = lax.all_to_all(sums, line, split_axis=0, concat_axis=0, tiled=True)  5.09 us
    all_to_all x1, waiting for transfers between devices, body(): lax.all_to_all(outgoing, 'x', split_axis=0, concat_axis=0, tiled=True)  5.04 us
  transfers between devices with their start and end apart: 10, of which 8 were waited for; matrix products, arithmetic and copies ran while one was open for 3% of the time, Pallas kernels for 3%

profile of v1, /device:TPU:1, one launch (start us, length us, event | category | flops | bytes accessed | tf_op | source)
XLA Modules:
  0.0 113.5 jit_solution(3695781629454044075)
XLA Ops:
  0.6 1.2 %copy-done = bf16[128,4096]{1,0:T(8,128)(2,1)S(1)} copy-done((bf16[128,4096]{1,0:T(8,128)(2,1)S(1)}, bf16[128,4096]{1,0:T(8,128)(2,1)}, u32[]{:S(2)}) %copy-start) | copy-done | bytes 1048600
  1.9 0.7 copy-done.7
  2.6 0.7 shard_map.137
  3.3 18.8 %collective-permute-start = (bf16[4,64,512]{2,1,0:T(8,128)(2,1)S(1)}, bf16[4,64,512]{2,1,0:T(8,128)(2,1)S(1)}, u32[]{:S(2)}, u32[]{:S(2)}) collective-permute-start(bf16[4,64,512]{2,1,0:T(8,128)(2,1)S(1)} %shard_map.137), channel_id=1, source_target_pairs={{64,128},{80,144},{96,160},{112,176},{192,16},{208,32},{224,48},{2... | collective-permute-start | bytes 786440 | tf_op jit(solution)/shard_map/ppermute | solution.py:233
  22.1 0.6 shard_map.138.grads_ref
  22.7 1.9 %collective-permute-start.1 = (bf16[128,256]{1,0:T(8,128)(2,1)S(1)}, bf16[128,256]{1,0:T(8,128)(2,1)S(1)}, u32[]{:S(2)}, u32[]{:S(2)}) collective-permute-start(bf16[128,256]{1,0:T(8,128)(2,1)S(1)} %shard_map.138.grads_ref), channel_id=1, source_target_pairs={{0,192},{64,128},{128,64},{192,0},{1,193},{65,129},{129,65},{193,1... | collective-permute-start | bytes 196616 | tf_op jit(solution)/shard_map/ppermute | solution.py:236
  24.6 1.5 %shard_map.139.filled_ref = bf16[4,256,512]{2,1,0:T(8,128)(2,1)} custom-call(s32[8,32]{1,0:T(8,128)S(1)} %bitcast.26, bf16[128,4096]{1,0:T(8,128)(2,1)S(1)} %copy-done.1, bf16[128,256]{1,0:T(8,128)(2,1)S(1)} %shard_map.138.grads_ref), custom_call_target="tpu_custom_call" | custom-call | tf_op jit(solution)/shard_map/pallas_call | solution.py:239
  26.1 3.3 %collective-permute-done.1.grads_ref = bf16[128,256]{1,0:T(8,128)(2,1)S(1)} collective-permute-done((bf16[128,256]{1,0:T(8,128)(2,1)S(1)}, bf16[128,256]{1,0:T(8,128)(2,1)S(1)}, u32[]{:S(2)}, u32[]{:S(2)}) %collective-permute-start.1) | collective-permute-done | bytes 65568 | tf_op jit(solution)/shard_map/ppermute | solution.py:236
  29.5 0.9 shard_map.140
  30.4 4.2 %all-to-all-start = ((bf16[4,256,512]{2,1,0:T(8,128)(2,1)}), bf16[4,256,512]{2,1,0:T(8,128)(2,1)S(1)}, u32[]{:S(2)}, u32[]{:S(2)}) async-start(bf16[4,256,512]{2,1,0:T(8,128)(2,1)} %shard_map.140), calls=%async_computation | async-start | bytes 2097152 | tf_op jit(solution)/shard_map/all_to_all | solution.py:245
  34.6 1.9 %collective-permute-start.2 = (f32[128,512]{1,0:T(8,128)S(1)}, f32[128,512]{1,0:T(8,128)S(1)}, u32[]{:S(2)}, u32[]{:S(2)}) collective-permute-start(f32[128,512]{1,0:T(8,128)S(1)} %bitcast.21), channel_id=1, source_target_pairs={{0,64},{64,0},{128,192},{192,128},{1,65},{65,1},{129,193},{193,129... | collective-permute-start | bytes 786440 | tf_op jit(solution)/shard_map/ppermute | solution.py:15
  36.5 4.3 %collective-permute-start.3 = (f32[128,512]{1,0:T(8,128)S(1)}, f32[128,512]{1,0:T(8,128)S(1)}, u32[]{:S(2)}, u32[]{:S(2)}) collective-permute-start(f32[128,512]{1,0:T(8,128)S(1)} %bitcast.23), channel_id=1, source_target_pairs={{0,1},{1,0},{2,3},{3,2},{4,5},{5,4},{6,7},{7,6},{8,9},{9,8},{10,11... | collective-permute-start | bytes 786440 | tf_op jit(solution)/shard_map/ppermute | solution.py:15
  40.8 1.2 %collective-permute-done.2.other_ref = f32[128,512]{1,0:T(8,128)S(1)} collective-permute-done((f32[128,512]{1,0:T(8,128)S(1)}, f32[128,512]{1,0:T(8,128)S(1)}, u32[]{:S(2)}, u32[]{:S(2)}) %collective-permute-start.2) | collective-permute-done | bytes 262176 | tf_op jit(solution)/shard_map/ppermute | solution.py:15
  42.0 5.0 %all-to-all-done = bf16[4,256,512]{2,1,0:T(8,128)(2,1)S(1)} async-done(((bf16[4,256,512]{2,1,0:T(8,128)(2,1)}), bf16[4,256,512]{2,1,0:T(8,128)(2,1)S(1)}, u32[]{:S(2)}, u32[]{:S(2)}) %all-to-all-start) | async-done | bytes 1048608 | tf_op jit(solution)/shard_map/all_to_all | solution.py:245
  47.0 0.8 slice.11
  47.9 5.5 %collective-permute-start.4 = (bf16[512,512]{1,0:T(8,128)(2,1)}, bf16[512,512]{1,0:T(8,128)(2,1)S(1)}, u32[]{:S(2)}, u32[]{:S(2)}) collective-permute-start(bf16[512,512]{1,0:T(8,128)(2,1)} %bitcast.5), channel_id=1, source_target_pairs={{0,1},{1,0},{2,3},{3,2},{4,5},{5,4},{6,7},{7,6},{8,9},{9,8},{10,11... | collective-permute-start | bytes 1572872 | tf_op jit(solution)/shard_map/ppermute | solution.py:15
  53.4 1.7 %collective-permute-done.4 = bf16[512,512]{1,0:T(8,128)(2,1)S(1)} collective-permute-done((bf16[512,512]{1,0:T(8,128)(2,1)}, bf16[512,512]{1,0:T(8,128)(2,1)S(1)}, u32[]{:S(2)}, u32[]{:S(2)}) %collective-permute-start.4) | collective-permute-done | bytes 524320 | tf_op jit(solution)/shard_map/ppermute | solution.py:15
  55.8 1.9 %collective-permute-start.5 = (f32[256,512]{1,0:T(8,128)S(1)}, f32[256,512]{1,0:T(8,128)S(1)}, u32[]{:S(2)}, u32[]{:S(2)}) collective-permute-start(f32[256,512]{1,0:T(8,128)S(1)} %fusion), channel_id=1, source_target_pairs={{0,64},{64,0},{128,192},{192,128},{1,65},{65,1},{129,193},{193,129... | collective-permute-start | bytes 1572872 | tf_op jit(solution)/shard_map/ppermute | solution.py:15
  57.7 0.6 reduce_sum.18
  59.0 11.8 %collective-permute-done.5 = f32[256,512]{1,0:T(8,128)S(1)} collective-permute-done((f32[256,512]{1,0:T(8,128)S(1)}, f32[256,512]{1,0:T(8,128)S(1)}, u32[]{:S(2)}, u32[]{:S(2)}) %collective-permute-start.5) | collective-permute-done | bytes 524320 | tf_op jit(solution)/shard_map/ppermute | solution.py:15
  70.9 3.1 %collective-permute-start.6 = (f32[256,512]{1,0:T(8,128)S(1)}, f32[256,512]{1,0:T(8,128)S(1)}, u32[]{:S(2)}, u32[]{:S(2)}) collective-permute-start(f32[256,512]{1,0:T(8,128)S(1)} %add_divide_fusion.own_ref), channel_id=1, source_target_pairs={{0,1},{1,0},{2,3},{3,2},{4,5},{5,4},{6,7},{7,6},{8,9},{9,8},{10,11... | collective-permute-start | bytes 1572872 | tf_op jit(solution)/shard_map/ppermute | solution.py:15
  74.0 1.2 %shard_map.141 = (f32[256,256]{1,0:T(8,128)}, f32[256,256]{1,0:T(8,128)}, f32[1,128]{1,0:T(1,128)S(1)}, f32[256,512]{1,0:T(8,128)S(1)}, bf16[256,256]{1,0:T(8,128)(2,1)S(1)}, /*index=5*/bf16[256,256]{1,0:T(8,128)(2,1)S(1)}) custom-call(f32[256,512]{1,0:T(8,128)S(1)} %add_divide_fusion.own_ref, f32[256,256]{1,0:T(8,128)S(1)} %copy-done.2, ...), custom_call_target="tpu_custom_call" | custom-call | tf_op jit(solution)/shard_map/pallas_call | solution.py:265
  75.5 1.6 %shard_map.142 = (f32[256,256]{1,0:T(8,128)S(1)}, f32[64,2,128]{2,1,0:T(2,128)}) custom-call(f32[256,512]{1,0:T(8,128)S(1)} %get-tuple-element.21.inner_ref, f32[256,512]{1,0:T(8,128)S(1)} %collective-permute-done.6.other_ref, bf16[256,256]{1,0:T(8,128)(2,1)S(1)} %get-tuple-element.22.left_high_ref, bf16[256,256]{1,0:T(8,128)(2,1)S(1)} %get-tuple-element.23.left_low_ref, ...), custom_call_target="tpu_custom_call" | custom-call | tf_op jit(solution)/shard_map/pallas_call | solution.py:274
  77.1 8.6 %all-to-all-start.1 = ((f32[64,2,128]{2,1,0:T(2,128)}), f32[64,2,128]{2,1,0:T(2,128)S(1)}, u32[]{:S(2)}, u32[]{:S(2)}) async-start(f32[64,2,128]{2,1,0:T(2,128)} %get-tuple-element.26), calls=%async_computation.1 | async-start | bytes 131072 | tf_op jit(solution)/shard_map/all_to_all | solution.py:281
  85.8 9.8 %all-to-all-done.1 = f32[64,2,128]{2,1,0:T(2,128)S(1)} async-done(((f32[64,2,128]{2,1,0:T(2,128)}), f32[64,2,128]{2,1,0:T(2,128)S(1)}, u32[]{:S(2)}, u32[]{:S(2)}) %all-to-all-start.1) | async-done | bytes 65568 | tf_op jit(solution)/shard_map/all_to_all | solution.py:281
  95.6 0.6 broadcast_in_dim.9
  96.2 5.1 %all-to-all-start.2 = ((f32[16,2,128]{2,1,0:T(2,128)}), f32[16,2,128]{2,1,0:T(2,128)S(1)}, u32[]{:S(2)}, u32[]{:S(2)}) async-start(f32[16,2,128]{2,1,0:T(2,128)} %broadcast_in_dim.9), calls=%async_computation.2 | async-start | bytes 32768 | tf_op jit(solution)/shard_map/all_to_all | solution.py:284
  101.5 0.8 copy-done.10
  102.3 1.4 %fusion.4 = f32[1,1,128,512]{3,2,1,0:T(8,128)} fusion(f32[512,512]{1,0:T(8,128)S(1)} %maximum_select_fusion, f32[256,512]{1,0:T(8,128)S(1)} %add_divide_fusion.own_ref, s32[]{:T(128)S(6)} %select_n.42, f32[1,1,128,512]{3,2,1,0:T(8,128)S(1)} %copy-done.10), kind=kOutput, calls=%fused_computation.7 | convolution fusion | flops 201523200 | bytes 1835012 | tf_op jit(solution)/shard_map/dot_general | solution.py:297
  103.7 1.2 %fusion.2 = f32[1,1,128,512]{3,2,1,0:T(8,128)} fusion(f32[512,512]{1,0:T(8,128)S(1)} %maximum_select_fusion, s32[]{:T(128)S(6)} %select_n.45, f32[1,1,128,512]{3,2,1,0:T(8,128)S(1)} %copy-done.11), kind=kOutput, calls=%fused_computation.4 | convolution fusion | flops 201523200 | bytes 1835012 | tf_op jit(solution)/shard_map/dot_general | solution.py:300
  104.9 7.7 %all-to-all-done.2.sums_ref = f32[16,2,128]{2,1,0:T(2,128)S(1)} async-done(((f32[16,2,128]{2,1,0:T(2,128)}), f32[16,2,128]{2,1,0:T(2,128)S(1)}, u32[]{:S(2)}, u32[]{:S(2)}) %all-to-all-start.2) | async-done | bytes 16416 | tf_op jit(solution)/shard_map/all_to_all | solution.py:284
  112.6 0.9 shard_map.143
  (30 shorter events, 1.3 us)
Async XLA Ops:
  0.6 1.2 %copy-start = (bf16[128,4096]{1,0:T(8,128)(2,1)S(1)}, bf16[128,4096]{1,0:T(8,128)(2,1)}, u32[]{:S(2)}) copy-start(bf16[128,4096]{1,0:T(8,128)(2,1)} %feats_ref.3) | copy-start | bytes 3145732
  1.9 0.7 copy-start.7
  2.5 19.5 %copy-start.6 = (bf16[128,256]{1,0:T(8,128)(2,1)S(1)}, bf16[128,256]{1,0:T(8,128)(2,1)}, u32[]{:S(2)}) copy-start(bf16[128,256]{1,0:T(8,128)(2,1)} %grads_ref.1) | copy-start | bytes 196612
  2.5 19.5 %copy-start.9 = (s32[16]{0:T(128)S(1)}, s32[16]{0:T(128)}, u32[]{:S(2)}) copy-start(s32[16]{0:T(128)} %counts_ref.1) | copy-start | bytes 196
  2.5 22.0 %copy-start.1 = (bf16[128,4096]{1,0:T(8,128)(2,1)S(1)}, bf16[128,4096]{1,0:T(8,128)(2,1)}, u32[]{:S(2)}) copy-start(bf16[128,4096]{1,0:T(8,128)(2,1)} %feats_ref.3) | copy-start | bytes 3145732
  3.3 21.3 %copy-start.8 = (s32[32,8]{0,1:T(8,128)S(1)}, s32[32,8]{0,1:T(8,128)}, u32[]{:S(2)}) copy-start(s32[32,8]{0,1:T(8,128)} %param.13) | copy-start | bytes 3076
  3.3 26.2 %collective-permute-start = (bf16[4,64,512]{2,1,0:T(8,128)(2,1)S(1)}, bf16[4,64,512]{2,1,0:T(8,128)(2,1)S(1)}, u32[]{:S(2)}, u32[]{:S(2)}) collective-permute-start(bf16[4,64,512]{2,1,0:T(8,128)(2,1)S(1)} %shard_map.137), channel_id=1, source_target_pairs={{64,128},{80,144},{96,160},{112,176},{192,16},{208,32},{224,48},{2... | collective-permute-start | bytes 786440 | tf_op jit(solution)/shard_map/ppermute | solution.py:233
  22.7 6.8 %collective-permute-start.1 = (bf16[128,256]{1,0:T(8,128)(2,1)S(1)}, bf16[128,256]{1,0:T(8,128)(2,1)S(1)}, u32[]{:S(2)}, u32[]{:S(2)}) collective-permute-start(bf16[128,256]{1,0:T(8,128)(2,1)S(1)} %shard_map.138.grads_ref), channel_id=1, source_target_pairs={{0,192},{64,128},{128,64},{192,0},{1,193},{65,129},{129,65},{193,1... | collective-permute-start | bytes 196616 | tf_op jit(solution)/shard_map/ppermute | solution.py:236
  30.4 4.2 %copy-start.4 = (f32[1,1,128,512]{3,2,1,0:T(8,128)S(1)}, f32[1,1,128,512]{3,2,1,0:T(8,128)}, u32[]{:S(2)}) copy-start(f32[1,1,128,512]{3,2,1,0:T(8,128)} %param.18) | copy-start | bytes 786436
  30.4 6.1 %copy-start.5 = (f32[1,1,128,512]{3,2,1,0:T(8,128)S(1)}, f32[1,1,128,512]{3,2,1,0:T(8,128)}, u32[]{:S(2)}) copy-start(f32[1,1,128,512]{3,2,1,0:T(8,128)} %param.19) | copy-start | bytes 786436
  30.4 16.6 %all-to-all-start = ((bf16[4,256,512]{2,1,0:T(8,128)(2,1)}), bf16[4,256,512]{2,1,0:T(8,128)(2,1)S(1)}, u32[]{:S(2)}, u32[]{:S(2)}) async-start(bf16[4,256,512]{2,1,0:T(8,128)(2,1)} %shard_map.140), calls=%async_computation | async-start | bytes 2097152 | tf_op jit(solution)/shard_map/all_to_all | solution.py:245
  34.6 7.4 %collective-permute-start.2 = (f32[128,512]{1,0:T(8,128)S(1)}, f32[128,512]{1,0:T(8,128)S(1)}, u32[]{:S(2)}, u32[]{:S(2)}) collective-permute-start(f32[128,512]{1,0:T(8,128)S(1)} %bitcast.21), channel_id=1, source_target_pairs={{0,64},{64,0},{128,192},{192,128},{1,65},{65,1},{129,193},{193,129... | collective-permute-start | bytes 786440 | tf_op jit(solution)/shard_map/ppermute | solution.py:15
  36.5 5.5 %collective-permute-start.3 = (f32[128,512]{1,0:T(8,128)S(1)}, f32[128,512]{1,0:T(8,128)S(1)}, u32[]{:S(2)}, u32[]{:S(2)}) collective-permute-start(f32[128,512]{1,0:T(8,128)S(1)} %bitcast.23), channel_id=1, source_target_pairs={{0,1},{1,0},{2,3},{3,2},{4,5},{5,4},{6,7},{7,6},{8,9},{9,8},{10,11... | collective-permute-start | bytes 786440 | tf_op jit(solution)/shard_map/ppermute | solution.py:15
  47.9 7.2 %collective-permute-start.4 = (bf16[512,512]{1,0:T(8,128)(2,1)}, bf16[512,512]{1,0:T(8,128)(2,1)S(1)}, u32[]{:S(2)}, u32[]{:S(2)}) collective-permute-start(bf16[512,512]{1,0:T(8,128)(2,1)} %bitcast.5), channel_id=1, source_target_pairs={{0,1},{1,0},{2,3},{3,2},{4,5},{5,4},{6,7},{7,6},{8,9},{9,8},{10,11... | collective-permute-start | bytes 1572872 | tf_op jit(solution)/shard_map/ppermute | solution.py:15
  55.8 15.0 %collective-permute-start.5 = (f32[256,512]{1,0:T(8,128)S(1)}, f32[256,512]{1,0:T(8,128)S(1)}, u32[]{:S(2)}, u32[]{:S(2)}) collective-permute-start(f32[256,512]{1,0:T(8,128)S(1)} %fusion), channel_id=1, source_target_pairs={{0,64},{64,0},{128,192},{192,128},{1,65},{65,1},{129,193},{193,129... | collective-permute-start | bytes 1572872 | tf_op jit(solution)/shard_map/ppermute | solution.py:15
  59.0 15.0 %copy-start.2 = (f32[256,256]{1,0:T(8,128)S(1)}, f32[256,256]{1,0:T(8,128)}, u32[]{:S(2)}) copy-start(f32[256,256]{1,0:T(8,128)} %moment_ref.1) | copy-start | bytes 786436
  59.0 15.0 %copy-start.3 = (f32[256,256]{1,0:T(8,128)S(1)}, f32[256,256]{1,0:T(8,128)}, u32[]{:S(2)}) copy-start(f32[256,256]{1,0:T(8,128)} %second_ref.1) | copy-start | bytes 786436
  70.9 4.6 %collective-permute-start.6 = (f32[256,512]{1,0:T(8,128)S(1)}, f32[256,512]{1,0:T(8,128)S(1)}, u32[]{:S(2)}, u32[]{:S(2)}) collective-permute-start(f32[256,512]{1,0:T(8,128)S(1)} %add_divide_fusion.own_ref), channel_id=1, source_target_pairs={{0,1},{1,0},{2,3},{3,2},{4,5},{5,4},{6,7},{7,6},{8,9},{9,8},{10,11... | collective-permute-start | bytes 1572872 | tf_op jit(solution)/shard_map/ppermute | solution.py:15
  77.1 18.4 %all-to-all-start.1 = ((f32[64,2,128]{2,1,0:T(2,128)}), f32[64,2,128]{2,1,0:T(2,128)S(1)}, u32[]{:S(2)}, u32[]{:S(2)}) async-start(f32[64,2,128]{2,1,0:T(2,128)} %get-tuple-element.26), calls=%async_computation.1 | async-start | bytes 131072 | tf_op jit(solution)/shard_map/all_to_all | solution.py:281
  96.2 16.4 %all-to-all-start.2 = ((f32[16,2,128]{2,1,0:T(2,128)}), f32[16,2,128]{2,1,0:T(2,128)S(1)}, u32[]{:S(2)}, u32[]{:S(2)}) async-start(f32[16,2,128]{2,1,0:T(2,128)} %broadcast_in_dim.9), calls=%async_computation.2 | async-start | bytes 32768 | tf_op jit(solution)/shard_map/all_to_all | solution.py:284
  101.3 1.0 copy-start.10
  102.3 1.4 %copy-start.11 = (f32[1,1,128,512]{3,2,1,0:T(8,128)S(1)}, f32[1,1,128,512]{3,2,1,0:T(8,128)}, u32[]{:S(2)}) copy-start(f32[1,1,128,512]{3,2,1,0:T(8,128)} %param.17) | copy-start | bytes 786436

commit v2 on v1

--- a/solution.py
+++ b/solution.py
@@ -54,7 +54,7 @@
     ]
 
 
-def lend_kernel(order_ref, feats_ref, out_ref, sems):
+def lend_kernel(order_ref, feats_ref, after_ref, out_ref, sems):
     zl = lax.axis_index("zl")
     runs = lax.axis_size("zh")
     turn = jnp.where(zl == 3, 1, jnp.where(zl == 0, runs - 1, 0))
@@ -66,11 +66,11 @@
         copy.wait()
 
 
-def mask_kernel(counts_ref, grads_ref, out_ref):
+def masked_rows(counts_ref, grads_ref, zl):
     rows = lax.broadcasted_iota(jnp.int32, grads_ref.shape, 0)
-    count = counts_ref[lax.axis_index("x") * lax.axis_size("zl") + lax.axis_index("zl")]
+    count = counts_ref[lax.axis_index("x") * lax.axis_size("zl") + zl]
     masked = jnp.where(rows < count, grads_ref[...].astype(jnp.float32), 0.0)
-    out_ref[...] = masked.astype(jnp.bfloat16)
+    return masked.astype(jnp.bfloat16)
 
 
 def grads_copies(grads_ref, out_ref, sems, first):
@@ -87,24 +87,41 @@
     ]
 
 
-def own_kernel(order_ref, feats_ref, grads_ref, out_ref, sems, grads_sems):
+def own_kernel(
+    counts_ref,
+    order_ref,
+    feats_ref,
+    grads_ref,
+    lent_grads_ref,
+    out_ref,
+    own_ref,
+    lent_ref,
+    sems,
+    own_sems,
+    lent_sems,
+):
     half = feats_ref.shape[0] // 2
+    zl = lax.axis_index("zl")
     brow = lax.axis_index("zh") * lax.axis_size("y") + lax.axis_index("y")
-    copies = block_copies(order_ref, feats_ref, out_ref, sems, 0, brow, lax.axis_index("zl") // 2)
-    copies += grads_copies(grads_ref, out_ref, grads_sems, 2 * half)
+    copies = block_copies(order_ref, feats_ref, out_ref, sems, 0, brow, zl // 2)
     for copy in copies:
         copy.start()
-    for copy in copies:
+    own_ref[...] = masked_rows(counts_ref, grads_ref, zl)
+    lent_ref[...] = masked_rows(counts_ref, lent_grads_ref, 3 - zl)
+    others = grads_copies(own_ref, out_ref, own_sems, 2 * half)
+    others += grads_copies(lent_ref, out_ref, lent_sems, 3 * half)
+    for copy in others:
+        copy.start()
+    for copy in copies + others:
         copy.wait()
 
 
-def lent_kernel(feats_ref, grads_ref, filled_ref, out_ref, sems, grads_sems):
+def lent_kernel(feats_ref, filled_ref, out_ref, sems):
     half = feats_ref.shape[1]
     copies = [
         pltpu.make_async_copy(feats_ref.at[x], out_ref.at[x, pl.ds(half, half), :], sems.at[x])
         for x in range(out_ref.shape[0])
     ]
-    copies += grads_copies(grads_ref, out_ref, grads_sems, 3 * half)
     for copy in copies:
         copy.start()
     for copy in copies:
@@ -223,23 +240,22 @@
     half_rows = tok_rows // 2
     lines = lax.axis_size("x")
     order = owner_order.T
+    lent_grads = lax.ppermute(out_grads, "zl", [(i, 3 - i) for i in range(4)])
     lent = call(
         lend_kernel,
         jax.ShapeDtypeStruct((lines, half_rows, block_size), jnp.bfloat16),
-        [SM, ANY],
+        [SM, ANY, ANY],
         VM,
         [pltpu.SemaphoreType.DMA((lines,))],
-    )(order, features)
+    )(order, features, lent_grads)
     lent = lax.ppermute(lent, ("zl", "zh"), z_partners())
-    masked = jax.ShapeDtypeStruct(out_grads.shape, jnp.bfloat16)
-    grads = call(mask_kernel, masked, [SM, VM], VM)(token_counts, out_grads)
-    lent_grads = lax.ppermute(grads, "zl", [(i, 3 - i) for i in range(4)])
     packed = jax.ShapeDtypeStruct((lines, 4 * half_rows, block_size), jnp.bfloat16)
-    sems = [pltpu.SemaphoreType.DMA((lines,)), pltpu.SemaphoreType.DMA((lines, 2))]
-    filled = call(own_kernel, packed, [SM, ANY, VM], ANY, sems)(order, features, grads)
-    outgoing = call(lent_kernel, packed, [VM, VM, ANY], ANY, sems, {2: 0})(
-        lent, lent_grads, filled
-    )
+    buffer = pltpu.VMEM(out_grads.shape, jnp.bfloat16)
+    each, pairs = pltpu.SemaphoreType.DMA((lines,)), pltpu.SemaphoreType.DMA((lines, 2))
+    filled = call(
+        own_kernel, packed, [SM, SM, ANY, VM, VM], ANY, [buffer, buffer, each, pairs, pairs]
+    )(token_counts, order, features, out_grads, lent_grads)
+    outgoing = call(lent_kernel, packed, [VM, ANY], ANY, [each], {1: 0})(lent, filled)
     left_other = partner(left_mine, "zl")
     right_other = partner(right_mine, "c")
     arrived = lax.all_to_all(outgoing, "x", split_axis=0, concat_axis=0, tiled=True)

time: 114 us -> 118 us (1.035)
  starting transfers between devices: 55.3 us -> 59.1 us
    ppermute x1, starting transfers between devices: 1.92 us -> 8.45 us  [body(): lent_grads = lax.ppermute(out_grads, 'zl', [(i, 3 - i) for i in range(4)])]
    ppermute x1, starting transfers between devices: 18.8 us -> 15.5 us  [body(): lent = lax.ppermute(lent, ('zl', 'zh'), z_partners())]
    ppermute x1, waiting for transfers between devices: 0.01 us -> 3.06 us  [body(): lent = lax.ppermute(lent, ('zl', 'zh'), z_partners())]
    ppermute x1, waiting for transfers between devices: 3.33 us -> 1.85 us  [body(): lent_grads = lax.ppermute(out_grads, 'zl', [(i, 3 - i) for i in range(4)])]
    pallas_call x3 -> x2, Pallas kernels: 2.99 us -> 2.46 us  [the longest x1 1.72 us: body(): call(own_kernel, packed, [SM, SM, ANY, VM, VM], ANY, [buffer, buffer, eac...]
    unnamed x24 -> x20, local copies, waits for them, and re-layouts: 2.79 us -> 2.79 us
  transfers between devices with their start and end apart: 10 -> 10, of which waited for: 8 -> 10; matrix products, arithmetic and copies ran while one was open for 3% -> 3% of each run, Pallas kernels for 3% -> 3%
where the time goes in v2:
time: 118 us
  starting transfers between devices  59.1 us (50%)
  waiting for transfers between devices  41.7 us (35%)
  Pallas kernels  6.87 us (6%)
  local copies, waits for them, and re-layouts  4.23 us (4%)
  matrix products  3.25 us (3%)
  between operations  1.54 us (1%)
    ppermute x5, starting transfers between devices, partner(): lax.ppermute(value, axis, [(i, i ^ 1) for i in range(lax.axis_size(axis))])  17.4 us
    ppermute x1, starting transfers between devices, body(): lent = lax.ppermute(lent, ('zl', 'zh'), z_partners())  15.5 us
    ppermute x5, waiting for transfers between devices, partner(): lax.ppermute(value, axis, [(i, i ^ 1) for i in range(lax.axis_size(axis))])  14.9 us
    all_to_all x1, waiting for transfers between devices, body(): sums = lax.all_to_all(sums, near, split_axis=0, concat_axis=0, tiled=True)  9.76 us
    all_to_all x1, starting transfers between devices, body(): sums = lax.all_to_all(sums, near, split_axis=0, concat_axis=0, tiled=True)  8.63 us
    ppermute x1, starting transfers between devices, body(): lent_grads = lax.ppermute(out_grads, 'zl', [(i, 3 - i) for i in range(4)])  8.45 us
    all_to_all x1, waiting for transfers between devices, body(): sums = lax.all_to_all(sums, line, split_axis=0, concat_axis=0, tiled=True)  7.71 us
    all_to_all x1, starting transfers between devices, body(): sums = lax.all_to_all(sums, line, split_axis=0, concat_axis=0, tiled=True)  4.93 us
  transfers between devices with their start and end apart: 10, of which 10 were waited for; matrix products, arithmetic and copies ran while one was open for 3% of the time, Pallas kernels for 3%

profile of v2, /device:TPU:1, one launch (start us, length us, event | category | flops | bytes accessed | tf_op | source)
XLA Modules:
  0.0 117.6 jit_solution(480705961836537693)
XLA Ops:
  0.6 8.4 %collective-permute-start = (bf16[128,256]{1,0:T(8,128)(2,1)}, bf16[128,256]{1,0:T(8,128)(2,1)S(1)}, u32[]{:S(2)}, u32[]{:S(2)}) collective-permute-start(bf16[128,256]{1,0:T(8,128)(2,1)} %grads_ref.1), channel_id=1, source_target_pairs={{0,192},{64,128},{128,64},{192,0},{1,193},{65,129},{129,65},{193,1... | collective-permute-start | bytes 196616 | tf_op jit(solution)/shard_map/ppermute | solution.py:243
  9.1 1.9 %collective-permute-done.after_ref.lent_grads_ref = bf16[128,256]{1,0:T(8,128)(2,1)S(1)} collective-permute-done((bf16[128,256]{1,0:T(8,128)(2,1)}, bf16[128,256]{1,0:T(8,128)(2,1)S(1)}, u32[]{:S(2)}, u32[]{:S(2)}) %collective-permute-start) | collective-permute-done | bytes 65568 | tf_op jit(solution)/shard_map/ppermute | solution.py:243
  10.9 1.2 %copy-done = bf16[128,4096]{1,0:T(8,128)(2,1)S(1)} copy-done((bf16[128,4096]{1,0:T(8,128)(2,1)S(1)}, bf16[128,4096]{1,0:T(8,128)(2,1)}, u32[]{:S(2)}) %copy-start) | copy-done | bytes 1048600
  12.2 0.7 copy-done.6
  12.9 0.7 shard_map.137
  13.6 15.5 %collective-permute-start.1 = (bf16[4,64,512]{2,1,0:T(8,128)(2,1)S(1)}, bf16[4,64,512]{2,1,0:T(8,128)(2,1)S(1)}, u32[]{:S(2)}, u32[]{:S(2)}) collective-permute-start(bf16[4,64,512]{2,1,0:T(8,128)(2,1)S(1)} %shard_map.137), channel_id=1, source_target_pairs={{64,128},{80,144},{96,160},{112,176},{192,16},{208,32},{224,48},{2... | collective-permute-start | bytes 786440 | tf_op jit(solution)/shard_map/ppermute | solution.py:251
  29.1 1.7 %shard_map.138.filled_ref = bf16[4,256,512]{2,1,0:T(8,128)(2,1)} custom-call(s32[16]{0:T(128)S(1)} %copy-done.7, s32[8,32]{1,0:T(8,128)S(1)} %bitcast.26, bf16[128,4096]{1,0:T(8,128)(2,1)S(1)} %copy-done, bf16[128,256]{1,0:T(8,128)(2,1)S(1)} %copy-done.5, bf16[128,256]{1,0:T(8,128)(2,1)S(1)} %collective-permute-done.after_ref.lent_grads_ref), custom_call_target="tpu_custom_call" | custom-call | tf_op jit(solution)/shard_map/pallas_call | solution.py:255
  30.9 3.1 %collective-permute-done.1.feats_ref = bf16[4,64,512]{2,1,0:T(8,128)(2,1)S(1)} collective-permute-done((bf16[4,64,512]{2,1,0:T(8,128)(2,1)S(1)}, bf16[4,64,512]{2,1,0:T(8,128)(2,1)S(1)}, u32[]{:S(2)}, u32[]{:S(2)}) %collective-permute-start.1) | collective-permute-done | bytes 262176 | tf_op jit(solution)/shard_map/ppermute | solution.py:251
  33.9 0.7 shard_map.139
  34.7 4.2 %all-to-all-start = ((bf16[4,256,512]{2,1,0:T(8,128)(2,1)}), bf16[4,256,512]{2,1,0:T(8,128)(2,1)S(1)}, u32[]{:S(2)}, u32[]{:S(2)}) async-start(bf16[4,256,512]{2,1,0:T(8,128)(2,1)} %shard_map.139), calls=%async_computation | async-start | bytes 2097152 | tf_op jit(solution)/shard_map/all_to_all | solution.py:261
  38.8 1.9 %collective-permute-start.2 = (f32[128,512]{1,0:T(8,128)S(1)}, f32[128,512]{1,0:T(8,128)S(1)}, u32[]{:S(2)}, u32[]{:S(2)}) collective-permute-start(f32[128,512]{1,0:T(8,128)S(1)} %bitcast.21), channel_id=1, source_target_pairs={{0,64},{64,0},{128,192},{192,128},{1,65},{65,1},{129,193},{193,129... | collective-permute-start | bytes 786440 | tf_op jit(solution)/shard_map/ppermute | solution.py:15
  40.8 4.6 %collective-permute-start.3 = (f32[128,512]{1,0:T(8,128)S(1)}, f32[128,512]{1,0:T(8,128)S(1)}, u32[]{:S(2)}, u32[]{:S(2)}) collective-permute-start(f32[128,512]{1,0:T(8,128)S(1)} %bitcast.23), channel_id=1, source_target_pairs={{0,1},{1,0},{2,3},{3,2},{4,5},{5,4},{6,7},{7,6},{8,9},{9,8},{10,11... | collective-permute-start | bytes 786440 | tf_op jit(solution)/shard_map/ppermute | solution.py:15
  45.4 0.8 collective-permute-done.2.other_ref
  46.6 4.4 %all-to-all-done = bf16[4,256,512]{2,1,0:T(8,128)(2,1)S(1)} async-done(((bf16[4,256,512]{2,1,0:T(8,128)(2,1)}), bf16[4,256,512]{2,1,0:T(8,128)(2,1)S(1)}, u32[]{:S(2)}, u32[]{:S(2)}) %all-to-all-start) | async-done | bytes 1048608 | tf_op jit(solution)/shard_map/all_to_all | solution.py:261
  51.0 0.8 slice.11
  51.8 5.8 %collective-permute-start.4 = (bf16[512,512]{1,0:T(8,128)(2,1)}, bf16[512,512]{1,0:T(8,128)(2,1)S(1)}, u32[]{:S(2)}, u32[]{:S(2)}) collective-permute-start(bf16[512,512]{1,0:T(8,128)(2,1)} %bitcast.5), channel_id=1, source_target_pairs={{0,1},{1,0},{2,3},{3,2},{4,5},{5,4},{6,7},{7,6},{8,9},{9,8},{10,11... | collective-permute-start | bytes 1572872 | tf_op jit(solution)/shard_map/ppermute | solution.py:15
  57.7 1.7 %collective-permute-done.4 = bf16[512,512]{1,0:T(8,128)(2,1)S(1)} collective-permute-done((bf16[512,512]{1,0:T(8,128)(2,1)}, bf16[512,512]{1,0:T(8,128)(2,1)S(1)}, u32[]{:S(2)}, u32[]{:S(2)}) %collective-permute-start.4) | collective-permute-done | bytes 524320 | tf_op jit(solution)/shard_map/ppermute | solution.py:15
  60.0 1.9 %collective-permute-start.5 = (f32[256,512]{1,0:T(8,128)S(1)}, f32[256,512]{1,0:T(8,128)S(1)}, u32[]{:S(2)}, u32[]{:S(2)}) collective-permute-start(f32[256,512]{1,0:T(8,128)S(1)} %fusion), channel_id=1, source_target_pairs={{0,64},{64,0},{128,192},{192,128},{1,65},{65,1},{129,193},{193,129... | collective-permute-start | bytes 1572872 | tf_op jit(solution)/shard_map/ppermute | solution.py:15
  61.9 0.6 reduce_sum.18
  63.3 11.8 %collective-permute-done.5 = f32[256,512]{1,0:T(8,128)S(1)} collective-permute-done((f32[256,512]{1,0:T(8,128)S(1)}, f32[256,512]{1,0:T(8,128)S(1)}, u32[]{:S(2)}, u32[]{:S(2)}) %collective-permute-start.5) | collective-permute-done | bytes 524320 | tf_op jit(solution)/shard_map/ppermute | solution.py:15
  75.1 3.1 %collective-permute-start.6 = (f32[256,512]{1,0:T(8,128)S(1)}, f32[256,512]{1,0:T(8,128)S(1)}, u32[]{:S(2)}, u32[]{:S(2)}) collective-permute-start(f32[256,512]{1,0:T(8,128)S(1)} %add_divide_fusion.own_ref), channel_id=1, source_target_pairs={{0,1},{1,0},{2,3},{3,2},{4,5},{5,4},{6,7},{7,6},{8,9},{9,8},{10,11... | collective-permute-start | bytes 1572872 | tf_op jit(solution)/shard_map/ppermute | solution.py:15
  78.3 1.2 %shard_map.140 = (f32[256,256]{1,0:T(8,128)}, f32[256,256]{1,0:T(8,128)}, f32[1,128]{1,0:T(1,128)S(1)}, f32[256,512]{1,0:T(8,128)S(1)}, bf16[256,256]{1,0:T(8,128)(2,1)S(1)}, /*index=5*/bf16[256,256]{1,0:T(8,128)(2,1)S(1)}) custom-call(f32[256,512]{1,0:T(8,128)S(1)} %add_divide_fusion.own_ref, f32[256,256]{1,0:T(8,128)S(1)} %copy-done.1, ...), custom_call_target="tpu_custom_call" | custom-call | tf_op jit(solution)/shard_map/pallas_call | solution.py:281
  79.8 1.6 %shard_map.141 = (f32[256,256]{1,0:T(8,128)S(1)}, f32[64,2,128]{2,1,0:T(2,128)}) custom-call(f32[256,512]{1,0:T(8,128)S(1)} %get-tuple-element.21.inner_ref, f32[256,512]{1,0:T(8,128)S(1)} %collective-permute-done.6.other_ref, bf16[256,256]{1,0:T(8,128)(2,1)S(1)} %get-tuple-element.22.left_high_ref, bf16[256,256]{1,0:T(8,128)(2,1)S(1)} %get-tuple-element.23.left_low_ref, ...), custom_call_target="tpu_custom_call" | custom-call | tf_op jit(solution)/shard_map/pallas_call | solution.py:290
  81.4 8.6 %all-to-all-start.1 = ((f32[64,2,128]{2,1,0:T(2,128)}), f32[64,2,128]{2,1,0:T(2,128)S(1)}, u32[]{:S(2)}, u32[]{:S(2)}) async-start(f32[64,2,128]{2,1,0:T(2,128)} %get-tuple-element.26), calls=%async_computation.1 | async-start | bytes 131072 | tf_op jit(solution)/shard_map/all_to_all | solution.py:297
  90.0 9.8 %all-to-all-done.1 = f32[64,2,128]{2,1,0:T(2,128)S(1)} async-done(((f32[64,2,128]{2,1,0:T(2,128)}), f32[64,2,128]{2,1,0:T(2,128)S(1)}, u32[]{:S(2)}, u32[]{:S(2)}) %all-to-all-start.1) | async-done | bytes 65568 | tf_op jit(solution)/shard_map/all_to_all | solution.py:297
  99.9 0.6 broadcast_in_dim.9
  100.5 4.9 %all-to-all-start.2 = ((f32[16,2,128]{2,1,0:T(2,128)}), f32[16,2,128]{2,1,0:T(2,128)S(1)}, u32[]{:S(2)}, u32[]{:S(2)}) async-start(f32[16,2,128]{2,1,0:T(2,128)} %broadcast_in_dim.9), calls=%async_computation.2 | async-start | bytes 32768 | tf_op jit(solution)/shard_map/all_to_all | solution.py:300
  105.6 0.8 copy-done.8
  106.4 1.4 %fusion.4 = f32[1,1,128,512]{3,2,1,0:T(8,128)} fusion(f32[512,512]{1,0:T(8,128)S(1)} %maximum_select_fusion, f32[256,512]{1,0:T(8,128)S(1)} %add_divide_fusion.own_ref, s32[]{:T(128)S(6)} %select_n.42, f32[1,1,128,512]{3,2,1,0:T(8,128)S(1)} %copy-done.8), kind=kOutput, calls=%fused_computation.7 | convolution fusion | flops 201523200 | bytes 1835012 | tf_op jit(solution)/shard_map/dot_general | solution.py:313
  107.8 1.2 %fusion.2 = f32[1,1,128,512]{3,2,1,0:T(8,128)} fusion(f32[512,512]{1,0:T(8,128)S(1)} %maximum_select_fusion, s32[]{:T(128)S(6)} %select_n.45, f32[1,1,128,512]{3,2,1,0:T(8,128)S(1)} %copy-done.9), kind=kOutput, calls=%fused_computation.4 | convolution fusion | flops 201523200 | bytes 1835012 | tf_op jit(solution)/shard_map/dot_general | solution.py:316
  109.0 7.7 %all-to-all-done.2.sums_ref = f32[16,2,128]{2,1,0:T(2,128)S(1)} async-done(((f32[16,2,128]{2,1,0:T(2,128)}), f32[16,2,128]{2,1,0:T(2,128)S(1)}, u32[]{:S(2)}, u32[]{:S(2)}) %all-to-all-start.2) | async-done | bytes 16416 | tf_op jit(solution)/shard_map/all_to_all | solution.py:300
  116.7 0.9 shard_map.142
  (25 shorter events, 1.6 us)
Async XLA Ops:
  0.6 10.3 %collective-permute-start = (bf16[128,256]{1,0:T(8,128)(2,1)}, bf16[128,256]{1,0:T(8,128)(2,1)S(1)}, u32[]{:S(2)}, u32[]{:S(2)}) collective-permute-start(bf16[128,256]{1,0:T(8,128)(2,1)} %grads_ref.1), channel_id=1, source_target_pairs={{0,192},{64,128},{128,64},{192,0},{1,193},{65,129},{129,65},{193,1... | collective-permute-start | bytes 196616 | tf_op jit(solution)/shard_map/ppermute | solution.py:243
  10.9 1.2 %copy-start = (bf16[128,4096]{1,0:T(8,128)(2,1)S(1)}, bf16[128,4096]{1,0:T(8,128)(2,1)}, u32[]{:S(2)}) copy-start(bf16[128,4096]{1,0:T(8,128)(2,1)} %feats_ref.3) | copy-start | bytes 3145732
  12.2 0.7 copy-start.6
  12.8 16.3 %copy-start.5 = (bf16[128,256]{1,0:T(8,128)(2,1)S(1)}, bf16[128,256]{1,0:T(8,128)(2,1)}, u32[]{:S(2)}) copy-start(bf16[128,256]{1,0:T(8,128)(2,1)} %grads_ref.1) | copy-start | bytes 196612
  12.9 16.3 %copy-start.7 = (s32[16]{0:T(128)S(1)}, s32[16]{0:T(128)}, u32[]{:S(2)}) copy-start(s32[16]{0:T(128)} %counts_ref.1) | copy-start | bytes 196
  13.6 20.3 %collective-permute-start.1 = (bf16[4,64,512]{2,1,0:T(8,128)(2,1)S(1)}, bf16[4,64,512]{2,1,0:T(8,128)(2,1)S(1)}, u32[]{:S(2)}, u32[]{:S(2)}) collective-permute-start(bf16[4,64,512]{2,1,0:T(8,128)(2,1)S(1)} %shard_map.137), channel_id=1, source_target_pairs={{64,128},{80,144},{96,160},{112,176},{192,16},{208,32},{224,48},{2... | collective-permute-start | bytes 786440 | tf_op jit(solution)/shard_map/ppermute | solution.py:251
  34.7 4.2 %copy-start.3 = (f32[1,1,128,512]{3,2,1,0:T(8,128)S(1)}, f32[1,1,128,512]{3,2,1,0:T(8,128)}, u32[]{:S(2)}) copy-start(f32[1,1,128,512]{3,2,1,0:T(8,128)} %param.18) | copy-start | bytes 786436
  34.7 6.1 %copy-start.4 = (f32[1,1,128,512]{3,2,1,0:T(8,128)S(1)}, f32[1,1,128,512]{3,2,1,0:T(8,128)}, u32[]{:S(2)}) copy-start(f32[1,1,128,512]{3,2,1,0:T(8,128)} %param.19) | copy-start | bytes 786436
  34.7 16.3 %all-to-all-start = ((bf16[4,256,512]{2,1,0:T(8,128)(2,1)}), bf16[4,256,512]{2,1,0:T(8,128)(2,1)S(1)}, u32[]{:S(2)}, u32[]{:S(2)}) async-start(bf16[4,256,512]{2,1,0:T(8,128)(2,1)} %shard_map.139), calls=%async_computation | async-start | bytes 2097152 | tf_op jit(solution)/shard_map/all_to_all | solution.py:261
  38.8 7.4 %collective-permute-start.2 = (f32[128,512]{1,0:T(8,128)S(1)}, f32[128,512]{1,0:T(8,128)S(1)}, u32[]{:S(2)}, u32[]{:S(2)}) collective-permute-start(f32[128,512]{1,0:T(8,128)S(1)} %bitcast.21), channel_id=1, source_target_pairs={{0,64},{64,0},{128,192},{192,128},{1,65},{65,1},{129,193},{193,129... | collective-permute-start | bytes 786440 | tf_op jit(solution)/shard_map/ppermute | solution.py:15
  40.8 5.8 %collective-permute-start.3 = (f32[128,512]{1,0:T(8,128)S(1)}, f32[128,512]{1,0:T(8,128)S(1)}, u32[]{:S(2)}, u32[]{:S(2)}) collective-permute-start(f32[128,512]{1,0:T(8,128)S(1)} %bitcast.23), channel_id=1, source_target_pairs={{0,1},{1,0},{2,3},{3,2},{4,5},{5,4},{6,7},{7,6},{8,9},{9,8},{10,11... | collective-permute-start | bytes 786440 | tf_op jit(solution)/shard_map/ppermute | solution.py:15
  51.8 7.6 %collective-permute-start.4 = (bf16[512,512]{1,0:T(8,128)(2,1)}, bf16[512,512]{1,0:T(8,128)(2,1)S(1)}, u32[]{:S(2)}, u32[]{:S(2)}) collective-permute-start(bf16[512,512]{1,0:T(8,128)(2,1)} %bitcast.5), channel_id=1, source_target_pairs={{0,1},{1,0},{2,3},{3,2},{4,5},{5,4},{6,7},{7,6},{8,9},{9,8},{10,11... | collective-permute-start | bytes 1572872 | tf_op jit(solution)/shard_map/ppermute | solution.py:15
  60.0 15.0 %collective-permute-start.5 = (f32[256,512]{1,0:T(8,128)S(1)}, f32[256,512]{1,0:T(8,128)S(1)}, u32[]{:S(2)}, u32[]{:S(2)}) collective-permute-start(f32[256,512]{1,0:T(8,128)S(1)} %fusion), channel_id=1, source_target_pairs={{0,64},{64,0},{128,192},{192,128},{1,65},{65,1},{129,193},{193,129... | collective-permute-start | bytes 1572872 | tf_op jit(solution)/shard_map/ppermute | solution.py:15
  63.2 15.0 %copy-start.1 = (f32[256,256]{1,0:T(8,128)S(1)}, f32[256,256]{1,0:T(8,128)}, u32[]{:S(2)}) copy-start(f32[256,256]{1,0:T(8,128)} %moment_ref.1) | copy-start | bytes 786436
  63.2 15.0 %copy-start.2 = (f32[256,256]{1,0:T(8,128)S(1)}, f32[256,256]{1,0:T(8,128)}, u32[]{:S(2)}) copy-start(f32[256,256]{1,0:T(8,128)} %second_ref.1) | copy-start | bytes 786436
  75.1 4.6 %collective-permute-start.6 = (f32[256,512]{1,0:T(8,128)S(1)}, f32[256,512]{1,0:T(8,128)S(1)}, u32[]{:S(2)}, u32[]{:S(2)}) collective-permute-start(f32[256,512]{1,0:T(8,128)S(1)} %add_divide_fusion.own_ref), channel_id=1, source_target_pairs={{0,1},{1,0},{2,3},{3,2},{4,5},{5,4},{6,7},{7,6},{8,9},{9,8},{10,11... | collective-permute-start | bytes 1572872 | tf_op jit(solution)/shard_map/ppermute | solution.py:15
  81.4 18.4 %all-to-all-start.1 = ((f32[64,2,128]{2,1,0:T(2,128)}), f32[64,2,128]{2,1,0:T(2,128)S(1)}, u32[]{:S(2)}, u32[]{:S(2)}) async-start(f32[64,2,128]{2,1,0:T(2,128)} %get-tuple-element.26), calls=%async_computation.1 | async-start | bytes 131072 | tf_op jit(solution)/shard_map/all_to_all | solution.py:297
  100.5 16.2 %all-to-all-start.2 = ((f32[16,2,128]{2,1,0:T(2,128)}), f32[16,2,128]{2,1,0:T(2,128)S(1)}, u32[]{:S(2)}, u32[]{:S(2)}) async-start(f32[16,2,128]{2,1,0:T(2,128)} %broadcast_in_dim.9), calls=%async_computation.2 | async-start | bytes 32768 | tf_op jit(solution)/shard_map/all_to_all | solution.py:300
  105.4 1.0 copy-start.8
  106.4 1.4 %copy-start.9 = (f32[1,1,128,512]{3,2,1,0:T(8,128)S(1)}, f32[1,1,128,512]{3,2,1,0:T(8,128)}, u32[]{:S(2)}) copy-start(f32[1,1,128,512]{3,2,1,0:T(8,128)} %param.17) | copy-start | bytes 786436

commit v3 on v1

--- a/solution.py
+++ b/solution.py
@@ -117,7 +117,8 @@
 
 
 def moment_kernel(
-    own_ref,
+    own_low_ref,
+    own_high_ref,
     moment_ref,
     second_ref,
     mine_ref,
@@ -130,12 +131,14 @@
     low_ref,
     left_ref,
 ):
-    half = own_ref.shape[0]
-    quarter = half // 2
+    quarter = own_low_ref.shape[0]
+    half = quarter * 2
     side = lax.axis_index("c")
     part = lax.rem(lax.axis_index("zl"), 2)
     place = lambda i, n: pl.ds(pl.multiple_of(i * n, n), n)
-    tile = own_ref[:, place(part, half)]
+    columns = place(part, half)
+    tile = jnp.concatenate([own_low_ref[:, columns], own_high_ref[:, columns]], 0)
+    own = jnp.concatenate([own_low_ref[...], own_high_ref[...]], 0)
     new_moment = 0.9 * moment_ref[...] + 0.1 * tile
     new_second = 0.95 * second_ref[...] + 0.05 * tile * tile
     new_moment_ref[...] = new_moment
@@ -143,13 +146,14 @@
     sum_ref[...] = lane_sums(new_moment / (jnp.sqrt(new_second) + 1e-08))
     left_ref[place(part, quarter), :] = mine_ref[...]
     left_ref[place(1 - part, quarter), :] = other_ref[...]
-    inner_ref[...] = dot_plain(split(left_ref[:, place(side, half)]), split(own_ref[...]))
+    inner_ref[...] = dot_plain(split(left_ref[:, place(side, half)]), split(own))
     high_ref[...], low_ref[...] = split(left_ref[:, place(1 - side, half)])
 
 
 def step_kernel(
     inner_ref,
-    other_ref,
+    other_low_ref,
+    other_high_ref,
     left_high_ref,
     left_low_ref,
     right_mine_ref,
@@ -165,7 +169,8 @@
     right_ref[place(side, quarter), :] = right_mine_ref[...]
     right_ref[place(1 - side, quarter), :] = right_other_ref[...]
     left = (left_high_ref[...], left_low_ref[...])
-    inner = inner_ref[...] + dot_plain(left, split(other_ref[...]))
+    other = jnp.concatenate([other_low_ref[...], other_high_ref[...]], 0)
+    inner = inner_ref[...] + dot_plain(left, split(other))
     precond = dot_rows(split(inner), split(right_ref[...]))
     precond_ref[...] = precond
     sums = jnp.concatenate([sum_ref[...], lane_sums(precond)], 0)
@@ -253,11 +258,13 @@
     own_first = side_bit == 0
     grads_own = jnp.where(own_first, grads_low, grads_high)
     grads_other = jnp.where(own_first, grads_high, grads_low)
-    partial = jnp.dot(grads_own.T, feats_own, preferred_element_type=f32) + jnp.dot(
-        grads_other.T, feats_other, preferred_element_type=f32
-    )
-    own_half = (partial + partner(partial, "zl")) / token_total
-    other_half = partner(own_half, "c")
+    own_parts, other_parts = [], []
+    for at in (slice(0, quarter), slice(quarter, half_size)):
+        partial = jnp.dot(
+            grads_own[:, at].T, feats_own, preferred_element_type=f32
+        ) + jnp.dot(grads_other[:, at].T, feats_other, preferred_element_type=f32)
+        own_parts.append((partial + partner(partial, "zl")) / token_total)
+        other_parts.append(partner(own_parts[-1], "c"))
 
     tile = jax.ShapeDtypeStruct((half_size, half_size), f32)
     piece = jax.ShapeDtypeStruct((half_size, half_size), jnp.bfloat16)
@@ -265,21 +272,23 @@
     new_moment, new_second, direction_sum, inner, left_high, left_low = call(
         moment_kernel,
         (tile, tile, jax.ShapeDtypeStruct((1, 128), f32), rows, piece, piece),
-        [VM] * 5,
+        [VM] * 6,
         (VM,) * 6,
         [pltpu.VMEM(rows.shape, f32)],
-    )(own_half, moment, second, left_mine, left_other)
+    )(*own_parts, moment, second, left_mine, left_other)
     near = ("x", "y", "c")
     line = ("zl", "zh")
     precond, sums = call(
         step_kernel,
         (tile, jax.ShapeDtypeStruct((lax.axis_size(near), 2, 128), f32)),
-        [VM] * 7,
+        [VM] * 8,
         (VM,) * 2,
         [pltpu.VMEM(rows.shape, f32)],
-    )(inner, other_half, left_high, left_low, right_mine, right_other, direction_sum)
+    )(inner, *other_parts, left_high, left_low, right_mine, right_other, direction_sum)
     sums = lax.all_to_all(sums, near, split_axis=0, concat_axis=0, tiled=True)
-    sums, own_rows, other_rows = lax.optimization_barrier((sums, own_half, other_half))
+    sums, own_parts, other_parts = lax.optimization_barrier((sums, own_parts, other_parts))
+    own_rows = jnp.concatenate(own_parts, 0)
+    other_rows = jnp.concatenate(other_parts, 0)
     sums = jnp.broadcast_to(jnp.sum(sums, 0), (lax.axis_size(line), 2, 128))
     sums = lax.all_to_all(sums, line, split_axis=0, concat_axis=0, tiled=True)
     update = call(scale_kernel, tile, [VM, VM], VM)(sums, precond)

time: 114 us -> 112 us (0.982)
  waiting for transfers between devices: 40.8 us -> 32 us
  starting transfers between devices: 55.3 us -> 62.6 us
    ppermute x5 -> x7, waiting for transfers between devices: 14.9 us -> 6.2 us  [partner(): lax.ppermute(value, axis, [(i, i ^ 1) for i in range(lax.axis_size(axis))])]
    ppermute x5 -> x7, starting transfers between devices: 16.7 us -> 24.1 us  [partner(): lax.ppermute(value, axis, [(i, i ^ 1) for i in range(lax.axis_size(axis))])]
  transfers between devices with their start and end apart: 10 -> 12, of which waited for: 8 -> 8; matrix products, arithmetic and copies ran while one was open for 3% -> 4% of each run, Pallas kernels for 3% -> 3%
where the time goes in v3:
time: 112 us
  starting transfers between devices  62.6 us (56%)
  waiting for transfers between devices  32 us (29%)
  Pallas kernels  7.47 us (7%)
  matrix products  3.61 us (3%)
  local copies, waits for them, and re-layouts  3.44 us (3%)
  between operations  1.61 us (1%)
    ppermute x7, starting transfers between devices, partner(): lax.ppermute(value, axis, [(i, i ^ 1) for i in range(lax.axis_size(axis))])  24.1 us
    ppermute x1, starting transfers between devices, body(): lent = lax.ppermute(lent, ('zl', 'zh'), z_partners())  18.8 us
    all_to_all x1, waiting for transfers between devices, body(): sums = lax.all_to_all(sums, near, split_axis=0, concat_axis=0, tiled=True)  9.76 us
    all_to_all x1, starting transfers between devices, body(): sums = lax.all_to_all(sums, near, split_axis=0, concat_axis=0, tiled=True)  8.53 us
    all_to_all x1, waiting for transfers between devices, body(): sums = lax.all_to_all(sums, line, split_axis=0, concat_axis=0, tiled=True)  7.71 us
    ppermute x7, waiting for transfers between devices, partner(): lax.ppermute(value, axis, [(i, i ^ 1) for i in range(lax.axis_size(axis))])  6.2 us
    all_to_all x1, starting transfers between devices, body(): sums = lax.all_to_all(sums, line, split_axis=0, concat_axis=0, tiled=True)  5.09 us
    all_to_all x1, waiting for transfers between devices, body(): lax.all_to_all(outgoing, 'x', split_axis=0, concat_axis=0, tiled=True)  5.04 us
  transfers between devices with their start and end apart: 12, of which 8 were waited for; matrix products, arithmetic and copies ran while one was open for 4% of the time, Pallas kernels for 3%

profile of v3, /device:TPU:1, one launch (start us, length us, event | category | flops | bytes accessed | tf_op | source)
XLA Modules:
  0.0 111.7 jit_solution(2685885967828937313)
XLA Ops:
  0.6 1.2 %copy-done = bf16[128,4096]{1,0:T(8,128)(2,1)S(1)} copy-done((bf16[128,4096]{1,0:T(8,128)(2,1)S(1)}, bf16[128,4096]{1,0:T(8,128)(2,1)}, u32[]{:S(2)}) %copy-start) | copy-done | bytes 1048600
  1.9 0.7 copy-done.7
  2.6 0.7 shard_map.137
  3.3 18.8 %collective-permute-start = (bf16[4,64,512]{2,1,0:T(8,128)(2,1)S(1)}, bf16[4,64,512]{2,1,0:T(8,128)(2,1)S(1)}, u32[]{:S(2)}, u32[]{:S(2)}) collective-permute-start(bf16[4,64,512]{2,1,0:T(8,128)(2,1)S(1)} %shard_map.137), channel_id=1, source_target_pairs={{64,128},{80,144},{96,160},{112,176},{192,16},{208,32},{224,48},{2... | collective-permute-start | bytes 786440 | tf_op jit(solution)/shard_map/ppermute | solution.py:238
  22.7 1.9 %collective-permute-start.1 = (bf16[128,256]{1,0:T(8,128)(2,1)S(1)}, bf16[128,256]{1,0:T(8,128)(2,1)S(1)}, u32[]{:S(2)}, u32[]{:S(2)}) collective-permute-start(bf16[128,256]{1,0:T(8,128)(2,1)S(1)} %shard_map.138.grads_ref), channel_id=1, source_target_pairs={{0,192},{64,128},{128,64},{192,0},{1,193},{65,129},{129,65},{193,1... | collective-permute-start | bytes 196616 | tf_op jit(solution)/shard_map/ppermute | solution.py:241
  24.6 1.6 %shard_map.139.filled_ref = bf16[4,256,512]{2,1,0:T(8,128)(2,1)} custom-call(s32[8,32]{1,0:T(8,128)S(1)} %bitcast.25, bf16[128,4096]{1,0:T(8,128)(2,1)S(1)} %copy-done.1, bf16[128,256]{1,0:T(8,128)(2,1)S(1)} %shard_map.138.grads_ref), custom_call_target="tpu_custom_call" | custom-call | tf_op jit(solution)/shard_map/pallas_call | solution.py:244
  26.2 3.3 %collective-permute-done.1.grads_ref = bf16[128,256]{1,0:T(8,128)(2,1)S(1)} collective-permute-done((bf16[128,256]{1,0:T(8,128)(2,1)S(1)}, bf16[128,256]{1,0:T(8,128)(2,1)S(1)}, u32[]{:S(2)}, u32[]{:S(2)}) %collective-permute-start.1) | collective-permute-done | bytes 65568 | tf_op jit(solution)/shard_map/ppermute | solution.py:241
  29.5 0.9 shard_map.140
  30.5 4.2 %all-to-all-start = ((bf16[4,256,512]{2,1,0:T(8,128)(2,1)}), bf16[4,256,512]{2,1,0:T(8,128)(2,1)S(1)}, u32[]{:S(2)}, u32[]{:S(2)}) async-start(bf16[4,256,512]{2,1,0:T(8,128)(2,1)} %shard_map.140), calls=%async_computation | async-start | bytes 2097152 | tf_op jit(solution)/shard_map/all_to_all | solution.py:250
  34.6 1.9 %collective-permute-start.2 = (f32[128,512]{1,0:T(8,128)S(1)}, f32[128,512]{1,0:T(8,128)S(1)}, u32[]{:S(2)}, u32[]{:S(2)}) collective-permute-start(f32[128,512]{1,0:T(8,128)S(1)} %bitcast.20), channel_id=1, source_target_pairs={{0,64},{64,0},{128,192},{192,128},{1,65},{65,1},{129,193},{193,129... | collective-permute-start | bytes 786440 | tf_op jit(solution)/shard_map/ppermute | solution.py:15
  36.5 4.3 %collective-permute-start.3 = (f32[128,512]{1,0:T(8,128)S(1)}, f32[128,512]{1,0:T(8,128)S(1)}, u32[]{:S(2)}, u32[]{:S(2)}) collective-permute-start(f32[128,512]{1,0:T(8,128)S(1)} %bitcast.22), channel_id=1, source_target_pairs={{0,1},{1,0},{2,3},{3,2},{4,5},{5,4},{6,7},{7,6},{8,9},{9,8},{10,11... | collective-permute-start | bytes 786440 | tf_op jit(solution)/shard_map/ppermute | solution.py:15
  40.9 1.2 %collective-permute-done.2.other_ref = f32[128,512]{1,0:T(8,128)S(1)} collective-permute-done((f32[128,512]{1,0:T(8,128)S(1)}, f32[128,512]{1,0:T(8,128)S(1)}, u32[]{:S(2)}, u32[]{:S(2)}) %collective-permute-start.2) | collective-permute-done | bytes 262176 | tf_op jit(solution)/shard_map/ppermute | solution.py:15
  42.0 5.0 %all-to-all-done = bf16[4,256,512]{2,1,0:T(8,128)(2,1)S(1)} async-done(((bf16[4,256,512]{2,1,0:T(8,128)(2,1)}), bf16[4,256,512]{2,1,0:T(8,128)(2,1)S(1)}, u32[]{:S(2)}, u32[]{:S(2)}) %all-to-all-start) | async-done | bytes 1048608 | tf_op jit(solution)/shard_map/all_to_all | solution.py:250
  47.1 5.5 %collective-permute-start.4 = (bf16[512,512]{1,0:T(8,128)(2,1)S(1)}, bf16[512,512]{1,0:T(8,128)(2,1)S(1)}, u32[]{:S(2)}, u32[]{:S(2)}) collective-permute-start(bf16[512,512]{1,0:T(8,128)(2,1)S(1)} %bitcast.26), channel_id=1, source_target_pairs={{0,1},{1,0},{2,3},{3,2},{4,5},{5,4},{6,7},{7,6},{8,9},{9,8},{10,11... | collective-permute-start | bytes 1572872 | tf_op jit(solution)/shard_map/ppermute | solution.py:15
  53.2 1.0 collective-permute-done.4
  54.4 1.9 %collective-permute-start.5 = (f32[128,512]{1,0:T(8,128)S(1)}, f32[128,512]{1,0:T(8,128)S(1)}, u32[]{:S(2)}, u32[]{:S(2)}) collective-permute-start(f32[128,512]{1,0:T(8,128)S(1)} %convolution_add_fusion.1), channel_id=1, source_target_pairs={{0,64},{64,0},{128,192},{192,128},{1,65},{65,1},{129,193},{193,129... | collective-permute-start | bytes 786440 | tf_op jit(solution)/shard_map/ppermute | solution.py:15
  56.6 3.4 %collective-permute-start.6 = (f32[128,512]{1,0:T(8,128)S(1)}, f32[128,512]{1,0:T(8,128)S(1)}, u32[]{:S(2)}, u32[]{:S(2)}) collective-permute-start(f32[128,512]{1,0:T(8,128)S(1)} %convolution_add_fusion), channel_id=1, source_target_pairs={{0,64},{64,0},{128,192},{192,128},{1,65},{65,1},{129,193},{193,129... | collective-permute-start | bytes 786440 | tf_op jit(solution)/shard_map/ppermute | solution.py:15
  60.0 0.6 reduce_sum.18
  61.2 2.6 %collective-permute-done.5 = f32[128,512]{1,0:T(8,128)S(1)} collective-permute-done((f32[128,512]{1,0:T(8,128)S(1)}, f32[128,512]{1,0:T(8,128)S(1)}, u32[]{:S(2)}, u32[]{:S(2)}) %collective-permute-start.5) | collective-permute-done | bytes 262176 | tf_op jit(solution)/shard_map/ppermute | solution.py:15
  63.9 4.0 %collective-permute-start.7 = (f32[128,512]{1,0:T(8,128)S(1)}, f32[128,512]{1,0:T(8,128)S(1)}, u32[]{:S(2)}, u32[]{:S(2)}) collective-permute-start(f32[128,512]{1,0:T(8,128)S(1)} %add_divide_fusion.1.own_low_ref), channel_id=1, source_target_pairs={{0,1},{1,0},{2,3},{3,2},{4,5},{5,4},{6,7},{7,6},{8,9},{9,8},{10,11... | collective-permute-start | bytes 786440 | tf_op jit(solution)/shard_map/ppermute | solution.py:15
  67.9 1.5 %collective-permute-done.6 = f32[128,512]{1,0:T(8,128)S(1)} collective-permute-done((f32[128,512]{1,0:T(8,128)S(1)}, f32[128,512]{1,0:T(8,128)S(1)}, u32[]{:S(2)}, u32[]{:S(2)}) %collective-permute-start.6) | collective-permute-done | bytes 262176 | tf_op jit(solution)/shard_map/ppermute | solution.py:15
  69.5 3.1 %collective-permute-start.8 = (f32[128,512]{1,0:T(8,128)S(1)}, f32[128,512]{1,0:T(8,128)S(1)}, u32[]{:S(2)}, u32[]{:S(2)}) collective-permute-start(f32[128,512]{1,0:T(8,128)S(1)} %add_divide_fusion.own_high_ref), channel_id=1, source_target_pairs={{0,1},{1,0},{2,3},{3,2},{4,5},{5,4},{6,7},{7,6},{8,9},{9,8},{10,11... | collective-permute-start | bytes 786440 | tf_op jit(solution)/shard_map/ppermute | solution.py:15
  72.6 1.2 %shard_map.141 = (f32[256,256]{1,0:T(8,128)}, f32[256,256]{1,0:T(8,128)}, f32[1,128]{1,0:T(1,128)S(1)}, f32[256,512]{1,0:T(8,128)S(1)}, bf16[256,256]{1,0:T(8,128)(2,1)S(1)}, /*index=5*/bf16[256,256]{1,0:T(8,128)(2,1)S(1)}) custom-call(f32[128,512]{1,0:T(8,128)S(1)} %add_divide_fusion.1.own_low_ref, f32[128,512]{1,0:T(8,128)S(1)} %add_divide_fusion.own_high_ref, ...), custom_call_target="tpu_custom_call" | custom-call | tf_op jit(solution)/shard_map/pallas_call | solution.py:272
  73.8 1.6 %shard_map.142 = (f32[256,256]{1,0:T(8,128)S(1)}, f32[64,2,128]{2,1,0:T(2,128)}) custom-call(f32[256,512]{1,0:T(8,128)S(1)} %get-tuple-element.23.inner_ref, f32[128,512]{1,0:T(8,128)S(1)} %collective-permute-done.7.other_low_ref, f32[128,512]{1,0:T(8,128)S(1)} %collective-permute-done.8.other_high_ref, ...), custom_call_target="tpu_custom_call" | custom-call | tf_op jit(solution)/shard_map/pallas_call | solution.py:281
  75.4 8.5 %all-to-all-start.1 = ((f32[64,2,128]{2,1,0:T(2,128)}), f32[64,2,128]{2,1,0:T(2,128)S(1)}, u32[]{:S(2)}, u32[]{:S(2)}) async-start(f32[64,2,128]{2,1,0:T(2,128)} %get-tuple-element.28), calls=%async_computation.1 | async-start | bytes 131072 | tf_op jit(solution)/shard_map/all_to_all | solution.py:288
  84.0 9.8 %all-to-all-done.1 = f32[64,2,128]{2,1,0:T(2,128)S(1)} async-done(((f32[64,2,128]{2,1,0:T(2,128)}), f32[64,2,128]{2,1,0:T(2,128)S(1)}, u32[]{:S(2)}, u32[]{:S(2)}) %all-to-all-start.1) | async-done | bytes 65568 | tf_op jit(solution)/shard_map/all_to_all | solution.py:288
  94.4 5.1 %all-to-all-start.2 = ((f32[16,2,128]{2,1,0:T(2,128)}), f32[16,2,128]{2,1,0:T(2,128)S(1)}, u32[]{:S(2)}, u32[]{:S(2)}) async-start(f32[16,2,128]{2,1,0:T(2,128)} %broadcast_in_dim.9), calls=%async_computation.2 | async-start | bytes 32768 | tf_op jit(solution)/shard_map/all_to_all | solution.py:293
  99.7 0.8 copy-done.10
  100.5 1.4 %fusion.3 = f32[1,1,128,512]{3,2,1,0:T(8,128)} fusion(f32[512,512]{1,0:T(8,128)S(1)} %maximum_select_fusion, s32[]{:T(128)S(6)} %select_n.45, f32[128,512]{1,0:T(8,128)S(1)} %add_divide_fusion.1.own_low_ref, f32[128,512]{1,0:T(8,128)S(1)} %add_divide_fusion.own_high_ref, f32[1,1,128,512]{3,2,1,0:T(8,128)S(1)} %copy-done.10), kind=kOutput, calls=%fused_computation.7 | convolution fusion | flops 201588736 | bytes 2097156 | tf_op jit(solution)/shard_map/dot_general | solution.py:306
  101.9 1.2 %fusion.1 = f32[1,1,128,512]{3,2,1,0:T(8,128)} fusion(f32[512,512]{1,0:T(8,128)S(1)} %maximum_select_fusion, s32[]{:T(128)S(6)} %select_n.48, f32[1,1,128,512]{3,2,1,0:T(8,128)S(1)} %copy-done.11), kind=kOutput, calls=%fused_computation.4 | convolution fusion | flops 201523200 | bytes 1835012 | tf_op jit(solution)/shard_map/dot_general | solution.py:309
  103.1 7.7 %all-to-all-done.2.sums_ref = f32[16,2,128]{2,1,0:T(2,128)S(1)} async-done(((f32[16,2,128]{2,1,0:T(2,128)}), f32[16,2,128]{2,1,0:T(2,128)S(1)}, u32[]{:S(2)}, u32[]{:S(2)}) %all-to-all-start.2) | async-done | bytes 16416 | tf_op jit(solution)/shard_map/all_to_all | solution.py:293
  110.8 0.9 shard_map.143
  (37 shorter events, 2.6 us)
Async XLA Ops:
  0.6 1.2 %copy-start = (bf16[128,4096]{1,0:T(8,128)(2,1)S(1)}, bf16[128,4096]{1,0:T(8,128)(2,1)}, u32[]{:S(2)}) copy-start(bf16[128,4096]{1,0:T(8,128)(2,1)} %feats_ref.3) | copy-start | bytes 3145732
  1.9 0.7 copy-start.7
  2.5 19.5 %copy-start.6 = (bf16[128,256]{1,0:T(8,128)(2,1)S(1)}, bf16[128,256]{1,0:T(8,128)(2,1)}, u32[]{:S(2)}) copy-start(bf16[128,256]{1,0:T(8,128)(2,1)} %grads_ref.1) | copy-start | bytes 196612
  2.5 19.5 %copy-start.9 = (s32[16]{0:T(128)S(1)}, s32[16]{0:T(128)}, u32[]{:S(2)}) copy-start(s32[16]{0:T(128)} %counts_ref.1) | copy-start | bytes 196
  2.5 22.0 %copy-start.1 = (bf16[128,4096]{1,0:T(8,128)(2,1)S(1)}, bf16[128,4096]{1,0:T(8,128)(2,1)}, u32[]{:S(2)}) copy-start(bf16[128,4096]{1,0:T(8,128)(2,1)} %feats_ref.3) | copy-start | bytes 3145732
  3.3 21.3 %copy-start.8 = (s32[32,8]{0,1:T(8,128)S(1)}, s32[32,8]{0,1:T(8,128)}, u32[]{:S(2)}) copy-start(s32[32,8]{0,1:T(8,128)} %param.13) | copy-start | bytes 3076
  3.3 26.2 %collective-permute-start = (bf16[4,64,512]{2,1,0:T(8,128)(2,1)S(1)}, bf16[4,64,512]{2,1,0:T(8,128)(2,1)S(1)}, u32[]{:S(2)}, u32[]{:S(2)}) collective-permute-start(bf16[4,64,512]{2,1,0:T(8,128)(2,1)S(1)} %shard_map.137), channel_id=1, source_target_pairs={{64,128},{80,144},{96,160},{112,176},{192,16},{208,32},{224,48},{2... | collective-permute-start | bytes 786440 | tf_op jit(solution)/shard_map/ppermute | solution.py:238
  22.7 6.8 %collective-permute-start.1 = (bf16[128,256]{1,0:T(8,128)(2,1)S(1)}, bf16[128,256]{1,0:T(8,128)(2,1)S(1)}, u32[]{:S(2)}, u32[]{:S(2)}) collective-permute-start(bf16[128,256]{1,0:T(8,128)(2,1)S(1)} %shard_map.138.grads_ref), channel_id=1, source_target_pairs={{0,192},{64,128},{128,64},{192,0},{1,193},{65,129},{129,65},{193,1... | collective-permute-start | bytes 196616 | tf_op jit(solution)/shard_map/ppermute | solution.py:241
  30.4 4.2 %copy-start.4 = (f32[1,1,128,512]{3,2,1,0:T(8,128)S(1)}, f32[1,1,128,512]{3,2,1,0:T(8,128)}, u32[]{:S(2)}) copy-start(f32[1,1,128,512]{3,2,1,0:T(8,128)} %param.18) | copy-start | bytes 786436
  30.4 6.1 %copy-start.5 = (f32[1,1,128,512]{3,2,1,0:T(8,128)S(1)}, f32[1,1,128,512]{3,2,1,0:T(8,128)}, u32[]{:S(2)}) copy-start(f32[1,1,128,512]{3,2,1,0:T(8,128)} %param.19) | copy-start | bytes 786436
  30.5 16.6 %all-to-all-start = ((bf16[4,256,512]{2,1,0:T(8,128)(2,1)}), bf16[4,256,512]{2,1,0:T(8,128)(2,1)S(1)}, u32[]{:S(2)}, u32[]{:S(2)}) async-start(bf16[4,256,512]{2,1,0:T(8,128)(2,1)} %shard_map.140), calls=%async_computation | async-start | bytes 2097152 | tf_op jit(solution)/shard_map/all_to_all | solution.py:250
  34.6 7.4 %collective-permute-start.2 = (f32[128,512]{1,0:T(8,128)S(1)}, f32[128,512]{1,0:T(8,128)S(1)}, u32[]{:S(2)}, u32[]{:S(2)}) collective-permute-start(f32[128,512]{1,0:T(8,128)S(1)} %bitcast.20), channel_id=1, source_target_pairs={{0,64},{64,0},{128,192},{192,128},{1,65},{65,1},{129,193},{193,129... | collective-permute-start | bytes 786440 | tf_op jit(solution)/shard_map/ppermute | solution.py:15
  36.5 5.5 %collective-permute-start.3 = (f32[128,512]{1,0:T(8,128)S(1)}, f32[128,512]{1,0:T(8,128)S(1)}, u32[]{:S(2)}, u32[]{:S(2)}) collective-permute-start(f32[128,512]{1,0:T(8,128)S(1)} %bitcast.22), channel_id=1, source_target_pairs={{0,1},{1,0},{2,3},{3,2},{4,5},{5,4},{6,7},{7,6},{8,9},{9,8},{10,11... | collective-permute-start | bytes 786440 | tf_op jit(solution)/shard_map/ppermute | solution.py:15
  47.1 7.0 %collective-permute-start.4 = (bf16[512,512]{1,0:T(8,128)(2,1)S(1)}, bf16[512,512]{1,0:T(8,128)(2,1)S(1)}, u32[]{:S(2)}, u32[]{:S(2)}) collective-permute-start(bf16[512,512]{1,0:T(8,128)(2,1)S(1)} %bitcast.26), channel_id=1, source_target_pairs={{0,1},{1,0},{2,3},{3,2},{4,5},{5,4},{6,7},{7,6},{8,9},{9,8},{10,11... | collective-permute-start | bytes 1572872 | tf_op jit(solution)/shard_map/ppermute | solution.py:15
  54.4 9.4 %collective-permute-start.5 = (f32[128,512]{1,0:T(8,128)S(1)}, f32[128,512]{1,0:T(8,128)S(1)}, u32[]{:S(2)}, u32[]{:S(2)}) collective-permute-start(f32[128,512]{1,0:T(8,128)S(1)} %convolution_add_fusion.1), channel_id=1, source_target_pairs={{0,64},{64,0},{128,192},{192,128},{1,65},{65,1},{129,193},{193,129... | collective-permute-start | bytes 786440 | tf_op jit(solution)/shard_map/ppermute | solution.py:15
  56.6 12.8 %collective-permute-start.6 = (f32[128,512]{1,0:T(8,128)S(1)}, f32[128,512]{1,0:T(8,128)S(1)}, u32[]{:S(2)}, u32[]{:S(2)}) collective-permute-start(f32[128,512]{1,0:T(8,128)S(1)} %convolution_add_fusion), channel_id=1, source_target_pairs={{0,64},{64,0},{128,192},{192,128},{1,65},{65,1},{129,193},{193,129... | collective-permute-start | bytes 786440 | tf_op jit(solution)/shard_map/ppermute | solution.py:15
  63.9 8.7 %copy-start.2 = (f32[256,256]{1,0:T(8,128)S(1)}, f32[256,256]{1,0:T(8,128)}, u32[]{:S(2)}) copy-start(f32[256,256]{1,0:T(8,128)} %moment_ref.1) | copy-start | bytes 786436
  63.9 8.7 %copy-start.3 = (f32[256,256]{1,0:T(8,128)S(1)}, f32[256,256]{1,0:T(8,128)}, u32[]{:S(2)}) copy-start(f32[256,256]{1,0:T(8,128)} %second_ref.1) | copy-start | bytes 786436
  63.9 9.9 %collective-permute-start.7 = (f32[128,512]{1,0:T(8,128)S(1)}, f32[128,512]{1,0:T(8,128)S(1)}, u32[]{:S(2)}, u32[]{:S(2)}) collective-permute-start(f32[128,512]{1,0:T(8,128)S(1)} %add_divide_fusion.1.own_low_ref), channel_id=1, source_target_pairs={{0,1},{1,0},{2,3},{3,2},{4,5},{5,4},{6,7},{7,6},{8,9},{9,8},{10,11... | collective-permute-start | bytes 786440 | tf_op jit(solution)/shard_map/ppermute | solution.py:15
  69.5 4.4 %collective-permute-start.8 = (f32[128,512]{1,0:T(8,128)S(1)}, f32[128,512]{1,0:T(8,128)S(1)}, u32[]{:S(2)}, u32[]{:S(2)}) collective-permute-start(f32[128,512]{1,0:T(8,128)S(1)} %add_divide_fusion.own_high_ref), channel_id=1, source_target_pairs={{0,1},{1,0},{2,3},{3,2},{4,5},{5,4},{6,7},{7,6},{8,9},{9,8},{10,11... | collective-permute-start | bytes 786440 | tf_op jit(solution)/shard_map/ppermute | solution.py:15
  75.4 18.3 %all-to-all-start.1 = ((f32[64,2,128]{2,1,0:T(2,128)}), f32[64,2,128]{2,1,0:T(2,128)S(1)}, u32[]{:S(2)}, u32[]{:S(2)}) async-start(f32[64,2,128]{2,1,0:T(2,128)} %get-tuple-element.28), calls=%async_computation.1 | async-start | bytes 131072 | tf_op jit(solution)/shard_map/all_to_all | solution.py:288
  94.4 16.4 %all-to-all-start.2 = ((f32[16,2,128]{2,1,0:T(2,128)}), f32[16,2,128]{2,1,0:T(2,128)S(1)}, u32[]{:S(2)}, u32[]{:S(2)}) async-start(f32[16,2,128]{2,1,0:T(2,128)} %broadcast_in_dim.9), calls=%async_computation.2 | async-start | bytes 32768 | tf_op jit(solution)/shard_map/all_to_all | solution.py:293
  99.5 1.0 copy-start.10
  100.5 1.4 %copy-start.11 = (f32[1,1,128,512]{3,2,1,0:T(8,128)S(1)}, f32[1,1,128,512]{3,2,1,0:T(8,128)}, u32[]{:S(2)}) copy-start(f32[1,1,128,512]{3,2,1,0:T(8,128)} %param.17) | copy-start | bytes 786436
